TPU v7x, 256 devices: a whole 4x4x8 slice. The times are simulated.
256 devices in a mesh: tensor: 64 (over x, z, core), dp: 4 (over y).
Axes of the slice: x: 4, y: 4, z: 8, core: 2. Of those that a mesh axis runs over, the one named last changes fastest.
Arguments:
- tokens: bfloat16 [512, 8192], P('tensor', 'dp'), may hold values from -6 to 6
- gate_weight: bfloat16 [8192, 26624], P('dp', 'tensor'), may hold values from -0.0625 to 0.0625
- up_weight: bfloat16 [8192, 26624], P('dp', 'tensor'), may hold values from -0.0625 to 0.0625
- down_weight: bfloat16 [26624, 8192], P('tensor', 'dp'), may hold values from -6 to 6
- inverse_hessian: bfloat16 [26624, 26624], P(('tensor', 'dp')), may hold values from -2 to 3, as said below
- damping: float32 [26624], replicated, may hold values from 1 to 2.5
- removed: int32 [512], replicated, may hold values from 0 to 26623, as said below
Outputs:
- pruned_down: bfloat16 [26112, 8192], P('tensor', 'dp')
- mixed: bfloat16 [512, 8192], P('tensor', 'dp')
Inputs may be any that keep to these rules, and one draw needn't show every extreme that they name: `removed`: Strictly increasing. For every even t, the channels t * 416 to (t + 2) * 416 - 1 hold exactly 16 removed indices; the first half of them holds more than half of these when t // 2 is even and fewer when t // 2 is odd. Each aligned block of 104 channels holds at most 4 removed indices, and some block holds exactly 4. `inverse_hessian`: Symmetric; before its rounding to bfloat16 it is positive semidefinite.
All inputs are finite; a program needn't handle non-finite values.
Results may differ from a plain program's by a relative error of at most 0.0057.
Values may be sent and summed in bfloat16 or wider, within the bound.
A program may use at most 128 MiB of HBM per device.

v0:
```python
import jax
import jax.numpy as jnp
from jax import lax
from jax.sharding import PartitionSpec as P

FF = 26624
REM_DEV = 2
MOST = 4


def from_partner(value, axis, bit):
    mask = 2**bit
    pairs = [(source, source ^ mask) for source in range(lax.axis_size(axis))]
    return lax.ppermute(value, axis, pairs)


def solve_pair(factor, right_side):
    forward = lax.linalg.triangular_solve(factor, right_side, left_side=True, lower=True)
    return lax.linalg.triangular_solve(
        factor, forward, left_side=True, lower=True, transpose_a=True
    )


def gated_rows(values, width):
    return (jax.nn.silu(values[:, :width]) * values[:, width:]).astype(jnp.bfloat16)


def shards(tokens, gate_weight, up_weight, down_weight, inverse_hessian, damping, removed):
    tensor_size = lax.axis_size("tensor")
    group_size = lax.axis_size("dp")
    tensor_index = lax.axis_index("tensor")
    group_index = lax.axis_index("dp")
    shard_width = down_weight.shape[0]
    device_width = inverse_hessian.shape[0]
    removed_total = removed.shape[0]
    pair_quota = group_size * REM_DEV
    kept_width = shard_width - pair_quota
    device_index = tensor_index * group_size + group_index
    slot_range = jnp.arange(MOST, dtype=jnp.int32)
    owners = removed // device_width
    owner_first = jnp.searchsorted(removed, owners * device_width)
    compact = owners * MOST + jnp.arange(removed_total, dtype=jnp.int32) - owner_first
    device_first = jnp.searchsorted(removed, device_index * device_width)
    slot_channels = jnp.take(removed, device_first + slot_range, mode="clip")
    slot_local = jnp.clip(slot_channels - device_index * device_width, 0, device_width - 1)
    source_rows = jnp.take(inverse_hessian, slot_local, axis=0)
    block_piece = jnp.take(source_rows, removed, axis=1)
    block_all = lax.all_gather(block_piece, ("tensor", "dp"), axis=0, tiled=True)
    square = jnp.take(block_all, compact, axis=0).astype(jnp.float32) + jnp.diag(
        jnp.take(damping, removed)
    )
    square = 0.5 * (square + square.T)
    factor = jnp.linalg.cholesky(square)
    outgoing = source_rows.reshape(MOST, tensor_size, group_size, device_width).transpose(
        1, 2, 0, 3
    )
    arrived = lax.all_to_all(
        lax.all_to_all(outgoing, "tensor", split_axis=0, concat_axis=0, tiled=True),
        "dp",
        split_axis=1,
        concat_axis=1,
        tiled=True,
    )
    mine = jnp.take(arrived.reshape(-1, device_width), compact, axis=0).astype(jnp.float32)
    own_coef = solve_pair(factor, mine)
    coefficients = lax.all_gather(own_coef, "dp", axis=1, tiled=True)
    shard_first = jnp.searchsorted(removed, tensor_index * shard_width)
    shard_count = jnp.searchsorted(removed, (tensor_index + 1) * shard_width) - shard_first
    parity = tensor_index % 2
    even_count = jnp.where(parity == 0, shard_count, 2 * pair_quota - shard_count)
    sub_blocks = tensor_index * group_size + jnp.arange(group_size, dtype=jnp.int32)
    sub_first = jnp.searchsorted(removed, sub_blocks * device_width)
    sub_channels = jnp.take(removed, sub_first[:, None] + slot_range[None, :], mode="clip")
    sub_local = jnp.clip(sub_channels - tensor_index * shard_width, 0, shard_width - 1).reshape(-1)
    lost_local = jnp.take(down_weight, sub_local, axis=0)
    lost_every = lax.all_gather(lost_local, "tensor", axis=0, tiled=True)
    lost_rows = jnp.take(lost_every, compact, axis=0)
    local_channels = tensor_index * shard_width + jnp.arange(shard_width, dtype=jnp.int32)
    is_removed = jnp.any(local_channels[:, None] == removed[None, :], axis=1).astype(jnp.int32)
    kept_order = jnp.argsort(is_removed, stable=True)
    own_kept = shard_width - shard_count
    even_kept = shard_width - even_count
    slab_index = jnp.where(parity == 0, kept_order[kept_width:], kept_order[:pair_quota])
    kept_places = jnp.arange(kept_width, dtype=jnp.int32)
    even_pack = jnp.where(
        kept_places < own_kept, kept_order[:kept_width], shard_width + kept_places - own_kept
    )
    odd_source = jnp.take(
        kept_order, jnp.clip(kept_width + kept_places - even_kept, 0, shard_width - 1)
    )
    odd_pack = jnp.where(
        kept_width + kept_places < even_kept, shard_width + kept_places, odd_source
    )
    pack_index = jnp.where(parity == 0, even_pack, odd_pack)
    input_slabs = jnp.stack(
        [jnp.take(gate_weight, slab_index, axis=1), jnp.take(up_weight, slab_index, axis=1)]
    )
    input_arrived = from_partner(input_slabs, "tensor", 0)
    gate_kept = jnp.take(
        jnp.concatenate([gate_weight, input_arrived[0]], axis=1), pack_index, axis=1
    )
    up_kept = jnp.take(jnp.concatenate([up_weight, input_arrived[1]], axis=1), pack_index, axis=1)
    gate_up = jnp.concatenate([gate_kept, up_kept], axis=1)
    preact = jnp.dot(
        lax.all_gather(tokens, "tensor", axis=0, tiled=True),
        gate_up,
        preferred_element_type=jnp.float32,
    )
    summed = lax.psum(preact, "dp")
    hidden = gated_rows(summed, kept_width)
    correction = lax.dot_general(
        coefficients,
        lost_rows.astype(jnp.float32),
        (((0,), (0,)), ((), ())),
        precision=lax.Precision.HIGHEST,
    )
    compensated = (down_weight.astype(jnp.float32) - correction).astype(jnp.bfloat16)
    down_slab = jnp.take(compensated, slab_index, axis=0)
    down_arrived = from_partner(down_slab, "tensor", 0)
    pruned_down = jnp.take(jnp.concatenate([compensated, down_arrived], axis=0), pack_index, axis=0)
    output_factor = FF ** (-0.5)
    mixed = lax.psum_scatter(
        jnp.dot(hidden, pruned_down, preferred_element_type=jnp.float32) * output_factor,
        "tensor",
        scatter_dimension=0,
        tiled=True,
    )
    return (pruned_down, mixed.astype(jnp.bfloat16))


def solution(mesh):
    in_specs = (
        P("tensor", "dp"),
        P("dp", "tensor"),
        P("dp", "tensor"),
        P("tensor", "dp"),
        P(("tensor", "dp"), None),
        P(),
        P(),
    )
    out_specs = (P("tensor", "dp"), P("tensor", "dp"))
    return jax.shard_map(shards, mesh=mesh, in_specs=in_specs, out_specs=out_specs, check_vma=False)
```

profile of v0, /device:TPU:8, one launch (start us, length us, event | category | flops | bytes accessed | tf_op | source)
XLA Modules:
  0.0 591.8 jit_solution(14776593844045080367)
XLA Ops:
  7.2 20.4 %while.95 = (s32[]{:T(128)}, u32[]{:T(128)}, u32[]{:T(128)}, s32[512]{0:T(512)}, s32[]{:T(128)}, /*index=5*/s32[]{:T(128)}, u32[]{:T(128)}) while((s32[]{:T(128)}, u32[]{:T(128)}, u32[]{:T(128)}, s32[512]{0:T(512)}, s32[]{:T(128)}, /*index=5*/s32[]{:T(128)}, u32[]{:T(128)}) %tuple.161), condition=%wide.region_9.10_spmd, body=%wide.region_8.9_spmd.sunk | while | flops 8 | bytes 160 | solution.py:43
  34.1 5.0 copy.23
  39.2 4.9 gather_fusion.5
  48.7 7.0 %while.98 = (s32[]{:T(128)}, u32[4]{0:T(128)S(1)}, u32[4]{0:T(128)S(1)}, s32[512]{0:T(512)S(1)}, s32[]{:T(128)}, /*index=5*/s32[]{:T(128)}, s32[]{:T(128)}, s32[]{}) while((s32[]{:T(128)}, u32[4]{0:T(128)S(1)}, u32[4]{0:T(128)S(1)}, s32[512]{0:T(512)S(1)}, s32[]{:T(128)}, /*index=5*/s32[]{:T(128)}, s32[]{:T(128)}, s32[]{}) %tuple.189), condition=%wide.region_19.20_spmd.clone, body=%wide.region_18.19_spmd.clone.sunk | while | flops 1088 | bytes 4408 | solution.py:72
  61.2 11.9 %all-to-all-start = ((bf16[64,4,4,104]{3,1,2,0:T(4,128)(2,1)}), bf16[64,4,4,104]{3,1,2,0:T(4,128)(2,1)S(1)}, u32[]{:S(2)}, u32[]{:S(2)}) async-start(bf16[64,4,4,104]{3,1,2,0:T(4,128)(2,1)} %fusion.21), calls=%async_computation | async-start | bytes 524288 | tf_op jit(solution)/shard_map/all_to_all | solution.py:58
  74.2 35.9 %while.97 = (s32[]{:T(128)}, u32[512]{0:T(512)S(1)}, u32[512]{0:T(512)S(1)}, s32[512]{0:T(512)S(1)}, s32[512]{0:T(512)S(1)}, /*index=5*/s32[]{:T(128)}, s32[]{:T(128)}, s32[]{}) while((s32[]{:T(128)}, u32[512]{0:T(512)S(1)}, u32[512]{0:T(512)S(1)}, s32[512]{0:T(512)S(1)}, s32[512]{0:T(512)S(1)}, /*index=5*/s32[]{:T(128)}, ...), condition=%wide.region_7.8_spmd.clone, body=%wide.region_6.7_spmd.clone.sunk | while | flops 10244 | bytes 40053 | solution.py:41
  110.7 13.6 %while.93 = (s32[]{:T(128)}, u32[]{:T(128)}, u32[]{:T(128)}, s32[512]{0:T(512)S(1)}, s32[]{:T(128)}, /*index=5*/s32[]{:T(128)}, u32[]{:T(128)}) while((s32[]{:T(128)}, u32[]{:T(128)}, u32[]{:T(128)}, s32[512]{0:T(512)S(1)}, s32[]{:T(128)}, /*index=5*/s32[]{:T(128)}, u32[]{:T(128)}) %tuple.191), condition=%wide.region_1.2_spmd, body=%wide.region_0.1_spmd.sunk | while | flops 8 | bytes 160 | solution.py:68
  124.3 13.9 %while.94 = (s32[]{:T(128)}, u32[]{:T(128)}, u32[]{:T(128)}, s32[512]{0:T(512)S(1)}, s32[]{:T(128)}, /*index=5*/s32[]{:T(128)}, u32[]{:T(128)}) while((s32[]{:T(128)}, u32[]{:T(128)}, u32[]{:T(128)}, s32[512]{0:T(512)S(1)}, s32[]{:T(128)}, /*index=5*/s32[]{:T(128)}, u32[]{:T(128)}) %tuple.192), condition=%wide.region_3.4_spmd, body=%wide.region_2.3_spmd.sunk | while | flops 8 | bytes 160 | solution.py:67
  147.7 4.9 all-to-all-start.1
  169.3 11.7 %cholesky.103 = f32[128,128]{1,0:T(8,128)S(1)} custom-call(f32[128,128]{1,0:T(8,128)S(1)} %cholesky.263), custom_call_target="Cholesky" | custom-call | tf_op jit(solution)/shard_map/jit(cholesky)/cholesky | solution.py:53
  181.2 9.8 %custom-call.32 = f32[1,128,128]{1,2,0:T(8,128)S(1)} custom-call(f32[1,128,128]{2,1,0:T(8,128)S(1)} %get-tuple-element.448), custom_call_target="InvertDiagBlocksLowerTriangular" | custom-call | tf_op jit(solution)/shard_map/jit(cholesky)/cholesky | solution.py:53
  193.5 11.7 %cholesky.215 = f32[128,128]{1,0:T(8,128)S(1)} custom-call(f32[128,128]{1,0:T(8,128)S(1)} %cholesky.267), custom_call_target="Cholesky" | custom-call | tf_op jit(solution)/shard_map/jit(cholesky)/cholesky | solution.py:53
  205.2 10.0 %custom-call.33 = f32[1,128,128]{1,2,0:T(8,128)S(1)} custom-call(f32[1,128,128]{2,1,0:T(8,128)S(1)} %get-tuple-element.445), custom_call_target="InvertDiagBlocksLowerTriangular" | custom-call | tf_op jit(solution)/shard_map/jit(cholesky)/cholesky | solution.py:53
  216.8 11.7 %cholesky.236 = f32[128,128]{1,0:T(8,128)S(1)} custom-call(f32[128,128]{1,0:T(8,128)S(1)} %cholesky.272), custom_call_target="Cholesky" | custom-call | tf_op jit(solution)/shard_map/jit(cholesky)/cholesky | solution.py:53
  228.5 9.8 %custom-call.34 = f32[1,128,128]{1,2,0:T(8,128)S(1)} custom-call(f32[1,128,128]{2,1,0:T(8,128)S(1)} %get-tuple-element.442), custom_call_target="InvertDiagBlocksLowerTriangular" | custom-call | tf_op jit(solution)/shard_map/jit(cholesky)/cholesky | solution.py:53
  239.9 11.7 %cholesky.253 = f32[128,128]{1,0:T(8,128)S(1)} custom-call(f32[128,128]{1,0:T(8,128)S(1)} %convolution_subtract_fusion.2), custom_call_target="Cholesky" | custom-call | tf_op jit(solution)/shard_map/jit(cholesky)/cholesky | solution.py:53
  257.4 13.5 %while.96 = (s32[]{:T(128)}, f32[512,512]{1,0:T(8,128)}, s32[4,2]{0,1:T(2,128)S(1)}, f32[4,128,128]{2,1,0:T(8,128)}, s32[]{:T(128)}) while((s32[]{:T(128)}, f32[512,512]{1,0:T(8,128)}, s32[4,2]{0,1:T(2,128)S(1)}, f32[4,128,128]{2,1,0:T(8,128)}, s32[]{:T(128)}) %tuple.167), condition=%wide.while_cond, body=%wide.while_body.sunk | while | flops 2 | bytes 132205 | solution.py:19
  270.9 40.1 %custom-call.35 = f32[4,128,128]{1,2,0:T(8,128)S(1)} custom-call(f32[4,128,128]{2,1,0:T(8,128)} %get-tuple-element.323), custom_call_target="InvertDiagBlocksLowerTriangular" | custom-call | tf_op jit(solution)/shard_map/triangular_solve | solution.py:19
  320.2 13.7 %all_gather.13 = f32[512,416]{0,1:T(8,128)S(1)} all-gather(f32[512,104]{0,1:T(8,128)S(1)} %pad_maximum_fusion.3), channel_id=1, replica_groups=mesh['tensor'=64,'dp'=4] {'dp'}, dimensions={1}, use_global_device_ids=true | all-gather | bytes 1064960 | tf_op jit(solution)/shard_map/all_gather | solution.py:66
  333.9 8.0 %gather_fusion.11 = bf16[512,2048]{1,0:T(8,128)(2,1)} fusion(bf16[1024,2048]{1,0:T(8,128)(2,1)} %all-gather.5.cloned.1.call-done, s32[1024]{0:T(1024)S(1)} %pad_clamp_fusion.6), kind=kCustom, calls=%fused_computation.15 | custom fusion | bytes 4196352 | tf_op jit(solution)/shard_map/jit(_take)/gather | solution.py:77
  341.9 6.0 %subtract_convert_fusion = bf16[416,2048]{1,0:T(8,128)(2,1)} fusion(bf16[416,2048]{1,0:T(8,128)(2,1)} %param.24, f32[512,416]{0,1:T(8,128)S(1)} %all_gather.13, bf16[512,2048]{1,0:T(8,128)(2,1)} %gather_fusion.11, pred[512]{0:T(512)(128)(4,1)S(1)} %copy-done.13), kind=kOutput, calls=%fused_computation.32 | convolution fusion | flops 5238095872 | bytes 6357504 | tf_op jit(solution)/shard_map/dot_general | solution.py:111
  370.0 6.3 %fusion.10 = f32[512,816]{0,1:T(8,128)} fusion(bf16[512,2048]{1,0:T(8,128)(2,1)} %all-gather.7.cloned.1.call-done, bf16[2048,408]{0,1:T(8,128)(2,1)} %get-tuple-element.452, bf16[2048,408]{0,1:T(8,128)(2,1)} %get-tuple-element.451), kind=kOutput, calls=%fused_computation.46 | convolution fusion | flops 1717960704 | bytes 7110656 | tf_op jit(solution)/shard_map/dot_general | solution.py:104
  376.3 57.3 %all-reduce.3.cloned.1.call-done = f32[512,816]{0,1:T(8,128)} async-done(((f32[512,816]{0,1:T(8,128)}), f32[512,816]{0,1:T(8,128)}) %all-reduce.3.cloned.1.call-update) | async-done | bytes 1671184 | tf_op jit(solution)/shard_map/psum | solution.py:109
  438.4 145.0 %reduce-scatter.2.cloned.1.call-done = f32[8,2048]{1,0:T(8,128)} async-done(((f32[512,2048]{1,0:T(8,128)}), f32[8,2048]{1,0:T(8,128)}) %reduce-scatter.2.cloned.1.call-update) | async-done | bytes 65552 | tf_op jit(solution)/shard_map/reduce_scatter | solution.py:122
  (300 shorter events, 172.6 us)
Async XLA Ops:
  7.2 36.9 %copy-start = (f32[26624]{0:T(1024)S(1)}, f32[26624]{0:T(1024)}, u32[]{:S(2)}) copy-start(f32[26624]{0:T(1024)} %param.26) | copy-start | bytes 319492
  7.2 154.3 %all-gather.9.cloned.1.call-start = ((), (), s32[]{:S(2)}) async-start(), calls=%async_computation.7 | async-start | bytes 1052672 | tf_op jit(solution)/shard_map/all_gather | solution.py:48
  39.2 8.0 %copy-start.1 = (s32[512]{0:T(512)S(1)}, s32[512]{0:T(512)}, u32[]{:S(2)}) copy-start(s32[512]{0:T(512)} %get-tuple-element.784) | copy-start | bytes 6148
  48.6 285.3 %all-gather.5.cloned.1.call-start = ((), (), s32[]{:S(2)}) async-start(), calls=%async_computation.3 | async-start | bytes 4259840 | tf_op jit(solution)/shard_map/all_gather | solution.py:76
  61.2 85.7 %all-to-all-start = ((bf16[64,4,4,104]{3,1,2,0:T(4,128)(2,1)}), bf16[64,4,4,104]{3,1,2,0:T(4,128)(2,1)S(1)}, u32[]{:S(2)}, u32[]{:S(2)}) async-start(bf16[64,4,4,104]{3,1,2,0:T(4,128)(2,1)} %fusion.21), calls=%async_computation | async-start | bytes 524288 | tf_op jit(solution)/shard_map/all_to_all | solution.py:58
  73.1 296.8 %all-gather.7.cloned.1.call-start = ((), (), s32[]{:S(2)}) async-start(), calls=%async_computation.4 | async-start | bytes 2129920 | tf_op jit(solution)/shard_map/all_gather | solution.py:105
  124.3 28.9 %copy-start.2 = (bf16[2048,416]{0,1:T(8,128)(2,1)S(1)}, bf16[2048,416]{0,1:T(8,128)(2,1)}, u32[]{:S(2)}) copy-start(bf16[2048,416]{0,1:T(8,128)(2,1)} %param.22) | copy-start | bytes 5111812
  147.7 10.5 %all-to-all-start.1 = ((bf16[64,4,4,104]{3,0,2,1:T(8,128)(2,1)}), bf16[64,4,4,104]{3,0,2,1:T(8,128)(2,1)}, u32[]{:S(2)}, u32[]{:S(2)}) async-start(bf16[64,4,4,104]{3,0,2,1:T(8,128)(2,1)} %copy.27), calls=%async_computation.1 | async-start | bytes 524288 | tf_op jit(solution)/shard_map/all_to_all | solution.py:57
  152.6 281.0 %all-reduce.3.cloned.1.call-start = ((), (), s32[]{:S(2)}) async-start(), calls=%async_computation.5 | async-start | bytes 3342336 | tf_op jit(solution)/shard_map/psum | solution.py:109
  153.2 1.5 copy-start.3
  156.1 4.7 copy-start.13
  165.3 2.7 copy-start.11
  215.5 41.9 %copy-start.16 = (s32[4]{0:T(128)S(1)}, s32[4]{0:T(128)}, u32[]{:S(2)}) copy-start(s32[4]{0:T(128)} %iota_multiply_fusion) | copy-start | bytes 52
  238.6 72.7 %copy-start.9 = (f32[512,104]{0,1:T(8,128)S(1)}, f32[512,104]{0,1:T(8,128)}, u32[]{:S(2)}) copy-start(f32[512,104]{0,1:T(8,128)} %get-tuple-element.427) | copy-start | bytes 638980
  341.9 8.5 %copy-start.5 = (bf16[8,2048]{1,0:T(8,128)(2,1)S(1)}, bf16[8,2048]{1,0:T(8,128)(2,1)}, u32[]{:S(2)}) copy-start(bf16[8,2048]{1,0:T(8,128)(2,1)} %gather_fusion.15) | copy-start | bytes 98308
  341.9 8.5 %copy-start.15 = (pred[8]{0:T(512)(128)(4,1)S(1)}, pred[8]{0:T(512)(128)(4,1)}, u32[]{:S(2)}) copy-start(pred[8]{0:T(512)(128)(4,1)} %get-tuple-element.425) | copy-start | bytes 28
  350.5 1.3 collective-permute-start
  351.2 2.1 copy-start.10
  351.2 5.6 collective-permute-start.1
  358.4 3.2 copy-start.4
  362.5 3.2 copy-start.6
  362.5 3.2 copy-start.14
  370.0 63.6 %copy-start.8 = (bf16[408,2048]{1,0:T(8,128)(2,1)}, bf16[408,2048]{1,0:T(8,128)(2,1)S(1)}, u32[]{:S(2)}) copy-start(bf16[408,2048]{1,0:T(8,128)(2,1)S(1)} %get-tuple-element.453) | copy-start | bytes 5013508
  376.3 207.1 %reduce-scatter.2.cloned.1.call-start = ((), (), s32[]{:S(2)}) async-start(), calls=%async_computation.6 | async-start | bytes 4259840 | tf_op jit(solution)/shard_map/reduce_scatter | solution.py:122
  (2 other events, 2.4 us)
Sparse Core Ops, SparseCore 0:
  48.8 105.4 all-gather.8
  157.1 78.5 all-gather.4
  238.5 75.4 all-gather.6
  376.4 57.1 all-reduce.2
  438.5 144.8 reduce-scatter.1
where the time goes:
time: 601 us; the launch traced here: 592 us
  waiting for transfers between devices  205 us (34%)
  other arithmetic  143 us (24%)
  local copies, waits for them, and re-layouts  142 us (24%)
  matrix products  31.6 us (5%)
  loops' own time  22.2 us (4%)
  starting transfers between devices  17.6 us (3%)
  between operations  17.4 us (3%)
  blocking collectives  13.7 us (2%)
    reduce_scatter x1, waiting for transfers between devices, shards(): lax.psum_scatter(jnp.dot(hidden, pruned_down, preferred_element_type=jnp....  145 us
    another operation x14, other arithmetic, shards(): factor = jnp.linalg.cholesky(square)  78.7 us
    psum x1, waiting for transfers between devices, shards(): summed = lax.psum(preact, 'dp')  57.3 us
    another operation x4, other arithmetic, solve_pair(): lax.linalg.triangular_solve(factor, forward, left_side=True, lower=True,...  41.8 us
    gather x10, local copies, waits for them, and re-layouts, shards(): owner_first = jnp.searchsorted(removed, owners * device_width)  34.9 us
    dynamic_slice x30, local copies, waits for them, and re-layouts, shards(): device_first = jnp.searchsorted(removed, device_index * device_width)  26.6 us
    all_gather x1, blocking collectives, shards(): coefficients = lax.all_gather(own_coef, 'dp', axis=1, tiled=True)  13.7 us
    another operation x12, local copies, waits for them, and re-layouts  13.5 us
  transfers between devices with their start and end apart: 9, of which 4 were waited for; matrix products, arithmetic and copies ran while one was open for 45% of the time, Pallas kernels for 0%

commit v1 on v0

v1 whole, which is shorter than its diff:
```python
import jax
import jax.numpy as jnp
from jax import lax
from jax.experimental import pallas as pl
from jax.experimental.pallas import tpu as pltpu
from jax.sharding import PartitionSpec as P

MESH = pl.DeviceIdType.MESH
BF = jnp.bfloat16
F32 = jnp.float32
NX, NZ, NY = 4, 8, 4
WIDTH = 416
BLOCK = 104
KEPT = 408
FF = 26624
REM = 512
STEPS = 8
VMEM_LIMIT = 52 * 1024 * 1024


def dot(a, b):
    return jnp.dot(a, b, preferred_element_type=F32)


def place():
    t = lax.axis_index("tensor")
    d = lax.axis_index("dp")
    return t // 16, (t // 2) % 8, t % 2, d


def at(x, z, c, d):
    return (x * 16 + z * 2 + c, d)


def remote(src, dst, send, recv, device):
    return pltpu.make_async_remote_copy(
        src_ref=src, dst_ref=dst, send_sem=send, recv_sem=recv, device_id=device, device_id_type=MESH
    )


def greet(devices):
    barrier = pltpu.get_barrier_semaphore()
    for device in devices:
        pl.semaphore_signal(barrier, inc=1, device_id=device, device_id_type=MESH)
    pl.semaphore_wait(barrier, len(devices))


def pair_indices(removed_s, pair):
    return [removed_s[pair * 16 + j] for j in range(16)]


def index_rows(indices, lanes):
    row = lax.broadcasted_iota(jnp.int32, (16, lanes), 0)
    out = jnp.full((16, lanes), -1, jnp.int32)
    for j, r in enumerate(indices):
        out = jnp.where(row == j, r, out)
    return out


def ranks(indices, first, lanes, rows=16):
    lane = lax.broadcasted_iota(jnp.int32, (rows, lanes), 1) + first
    shard = first
    below = jnp.zeros((rows, lanes), jnp.int32)
    gone = jnp.zeros((rows, lanes), jnp.int32)
    for r in indices:
        mine = jnp.where(r >= shard, 1, 0)
        below = below + jnp.where(r < lane, mine, 0)
        gone = gone + jnp.where(r == lane, 1, 0)
    return jnp.where(gone > 0, -1, lane - first - below)


def spread_kernel(
    removed_s, tok_ref, down_ref, damp_ref, removed_v, h_hbm,
    tok_o, l_o, s_o, hkr_o, slabd_o, slabh_o,
    hbuf, tokpad, lpad, spad, tok_rx, l_rx, s_rx, slabd_tx, slabh_tx,
    hsem, pair_s, pair_r, sc_s, sc_r, y_s, y_r, z_s, z_r, x_s, x_r, c_s, c_r, sl_s, sl_r,
):
    x, z, c, d = place()
    other = 1 - c
    pair = x * NZ + z
    first = (pair * 2 + c) * WIDTH
    quarter = FF // 4
    loads = [
        pltpu.make_async_copy(h_hbm.at[:, pl.ds(g * quarter, quarter)], hbuf.at[g], hsem.at[g]) for g in range(4)
    ]
    for load in loads:
        load.start()
    partner = at(x, z, other, d)
    right, left = at((x + 1) % NX, z, c, d), at((x + 3) % NX, z, c, d)
    ydev = [at(x, z, c, (d + k) % NY) for k in range(1, NY)]
    ycross = [at(x, z, other, (d + k) % NY) for k in range(1, NY)]
    zdev = [at(x, (z + k) % NZ, c, d) for k in range(1, NZ)]
    greet([partner, right, left] + ydev + ycross + zdev)

    indices = pair_indices(removed_s, pair)
    tok = tok_ref[...].astype(F32)
    none = jnp.zeros_like(tok)
    full = jnp.where(c == 0, jnp.concatenate([tok, none], axis=0), jnp.concatenate([none, tok], axis=0)).astype(BF)
    tokpad[0] = full[:, :1024]
    tokpad[1] = full[:, 1024:]
    tok_pair = remote(tokpad.at[other], tok_rx, pair_s.at[0], pair_r.at[0], partner)
    tok_pair.start()
    rows416 = index_rows(indices, WIDTH)
    lane416 = lax.broadcasted_iota(jnp.int32, (16, WIDTH), 1)
    pick = jnp.where(lane416 + first == rows416, 1.0, 0.0).astype(BF)
    lost = dot(pick, down_ref[...]).astype(BF)
    lpad[0] = lost[:, :1024]
    lpad[1] = lost[:, 1024:]
    l_pair = remote(lpad.at[other], l_rx, pair_s.at[1], pair_r.at[1], partner)
    l_pair.start()
    rank416 = ranks(indices, first, WIDTH)
    row16 = lax.broadcasted_iota(jnp.int32, (16, WIDTH), 0)
    target = jnp.where(row16 < 8, row16 + (1 - c) * KEPT, -7)
    slab_pick = jnp.where(rank416 == target, 1.0, 0.0)
    slabd_tx[...] = dot(slab_pick.astype(BF), down_ref[...]).astype(BF)
    slabd = remote(slabd_tx, slabd_o, sl_s.at[0], sl_r.at[0], partner)
    slabd.start()

    tok_pair.wait_recv()
    tok_o[c, x, z] = tokpad[c] + tok_rx[...]

    def z_sends(array, n):
        copies = [
            remote(array.at[c, x, z], array.at[c, x, z], z_s.at[n, k], z_r.at[n, k], zdev[k]) for k in range(NZ - 1)
        ]
        for copy in copies:
            copy.start()
        return copies

    tok_z = z_sends(tok_o, 0)
    l_pair.wait_recv()
    l_o[c, x, z] = lpad[c] + l_rx[...]
    l_z = z_sends(l_o, 1)

    chunk = quarter // 4
    for g in range(4):
        loads[g].wait()
        wanted = removed_v[:, g * 128 : (g + 1) * 128]
        total = jnp.zeros((BLOCK, 128), F32)
        for q in range(4):
            start = g * quarter + q * chunk
            channel = lax.broadcasted_iota(jnp.int32, (chunk, 128), 0) + start
            hot = jnp.where(channel == wanted, 1.0, 0.0).astype(BF)
            total = total + dot(hbuf[g, :, q * chunk : (q + 1) * chunk], hot)
        hkr_o[d, :, g * 128 : (g + 1) * 128] = total.astype(BF)
    rows104 = index_rows(indices, BLOCK)
    lane104 = lax.broadcasted_iota(jnp.int32, (16, BLOCK), 1)
    pick104 = jnp.where(lane104 + (first + d * BLOCK) == rows104, 1.0, 0.0)
    own_rows = dot(pick104.astype(BF), hkr_o[d]).astype(BF)
    damp = jnp.sum(pick104 * damp_ref[...], axis=1, keepdims=True)
    high = damp.astype(BF).astype(F32)
    lane128 = lax.broadcasted_iota(jnp.int32, (16, 128), 1)
    extra = jnp.where(lane128 == 0, high, jnp.where(lane128 == 1, damp - high, 0.0)).astype(BF)
    for half in range(2):
        spad[half, :, :256] = own_rows[:, half * 256 : (half + 1) * 256]
        spad[half, :, 256:] = extra
    s_sends = []
    for k in range(NY - 1):
        s_sends.append(remote(spad.at[c], s_rx.at[k], sc_s.at[k], sc_r.at[k], ydev[k]))
        s_sends.append(remote(spad.at[other], s_rx.at[3 + k], sc_s.at[3 + k], sc_r.at[3 + k], ycross[k]))
    s_sends.append(remote(spad.at[other], s_rx.at[6], sc_s.at[6], sc_r.at[6], partner))
    for copy in s_sends:
        copy.start()
    h_sends = [remote(hkr_o.at[d], hkr_o.at[d], y_s.at[k], y_r.at[k], ydev[k]) for k in range(NY - 1)]
    for copy in h_sends:
        copy.start()

    def x_sends(array, n):
        copies = [
            remote(array.at[c, x], array.at[c, x], x_s.at[n, 0], x_r.at[n, 0], right),
            remote(array.at[c, x], array.at[c, x], x_s.at[n, 1], x_r.at[n, 1], left),
        ]
        for copy in copies:
            copy.start()
        return copies

    def x_forwards(array, n):
        copies = [
            remote(
                array.at[c, (x + 3) % NX, pl.ds(0, 4)], array.at[c, (x + 3) % NX, pl.ds(0, 4)],
                x_s.at[n, 2], x_r.at[n, 2], right,
            ),
            remote(
                array.at[c, (x + 1) % NX, pl.ds(4, 4)], array.at[c, (x + 1) % NX, pl.ds(4, 4)],
                x_s.at[n, 3], x_r.at[n, 3], left,
            ),
        ]
        for copy in copies:
            copy.start()
        return copies

    def core_send(array, n, k):
        copy = remote(
            array.at[c, (x + k) % NX], array.at[c, (x + k) % NX], c_s.at[n, k], c_r.at[n, k], partner
        )
        copy.start()
        return copy

    started = []

    def stage_z(copies):
        for copy in copies:
            copy.wait_recv()

    stage_z(tok_z)
    tok_x = x_sends(tok_o, 0)
    tok_c = [core_send(tok_o, 0, 0)]
    for copy in s_sends:
        copy.wait_recv()
    total = spad[c].astype(F32)
    for k in range(7):
        total = total + s_rx[k].astype(F32)
    s_o[c, x, z] = total.astype(BF)
    s_z = z_sends(s_o, 2)
    stage_z(l_z)
    stage_z(s_z)
    s_x = x_sends(s_o, 2)
    s_c = [core_send(s_o, 2, 0)]
    stage_z(tok_x)
    tok_f = x_forwards(tok_o, 0)
    tok_c += [core_send(tok_o, 0, 1), core_send(tok_o, 0, 3)]
    l_x = x_sends(l_o, 1)
    l_c = [core_send(l_o, 1, 0)]
    stage_z(s_x)
    s_f = x_forwards(s_o, 2)
    s_c += [core_send(s_o, 2, 1), core_send(s_o, 2, 3)]
    stage_z(h_sends)
    slab = jnp.zeros((16, REM), F32)
    for k in range(NY):
        piece = jnp.where(ranks_piece(indices, first, k * BLOCK) == target[:, :BLOCK], 1.0, 0.0).astype(BF)
        slab = slab + dot(piece, hkr_o[k])
    slabh_tx[...] = slab.astype(BF)
    slabh = remote(slabh_tx, slabh_o, sl_s.at[1], sl_r.at[1], partner)
    slabh.start()
    stage_z(tok_f)
    tok_c.append(core_send(tok_o, 0, 2))
    stage_z(l_x)
    l_f = x_forwards(l_o, 1)
    l_c += [core_send(l_o, 1, 1), core_send(l_o, 1, 3)]
    stage_z(s_f)
    s_c.append(core_send(s_o, 2, 2))
    stage_z(l_f)
    l_c.append(core_send(l_o, 1, 2))
    stage_z(tok_c + s_c + l_c + [slabd, slabh])
    for copy in (
        [tok_pair, l_pair, slabd, slabh] + tok_z + l_z + s_z + s_sends + h_sends
        + tok_x + tok_f + tok_c + s_x + s_f + s_c + l_x + l_f + l_c
    ):
        copy.wait_send()


def ranks_piece(indices, first, offset):
    lane = lax.broadcasted_iota(jnp.int32, (16, BLOCK), 1) + (first + offset)
    below = jnp.zeros((16, BLOCK), jnp.int32)
    gone = jnp.zeros((16, BLOCK), jnp.int32)
    for r in indices:
        mine = jnp.where(r >= first, 1, 0)
        below = below + jnp.where(r < lane, mine, 0)
        gone = gone + jnp.where(r == lane, 1, 0)
    return jnp.where(gone > 0, -1, lane - first - below)


def hidden_kernel(removed_s, tok_ref, gate_ref, up_ref, hid_o, tx, rx, own, s_s, s_r, h_s, h_r):
    x, z, c, d = place()
    ydev = [at(x, z, c, (d + k) % NY) for k in range(1, NY)]
    greet(ydev)
    pair = x * NZ + z
    first = (pair * 2 + c) * WIDTH

    def partial(block, weight):
        total = dot(tok_ref[0, block], weight[:1024])
        return total + dot(tok_ref[1, block], weight[1024:])

    sends = []
    for k in range(1, NY):
        block = (d + k) % NY
        tx[k - 1, 0] = partial(block, gate_ref).astype(BF)
        tx[k - 1, 1] = partial(block, up_ref).astype(BF)
        copy = remote(tx.at[k - 1], rx.at[k - 1], s_s.at[k - 1], s_r.at[k - 1], ydev[k - 1])
        copy.start()
        sends.append(copy)
    own[0] = partial(d, gate_ref)
    own[1] = partial(d, up_ref)
    lane = lax.broadcasted_iota(jnp.int32, (8, WIDTH), 1) + first
    keep = jnp.ones((8, WIDTH), F32)
    for r in pair_indices(removed_s, pair):
        keep = jnp.where(lane == r, 0.0, keep)
    for copy in sends:
        copy.wait_recv()
    gate = own[0]
    up = own[1]
    for k in range(NY - 1):
        gate = gate + rx[k, 0].astype(F32)
        up = up + rx[k, 1].astype(F32)
    hidden = gate / (1.0 + jnp.exp(-gate)) * up
    hid_o[d] = jnp.where(keep[:1] > 0.0, hidden, 0.0).astype(BF)
    shares = [remote(hid_o.at[d], hid_o.at[d], h_s.at[k], h_r.at[k], ydev[k]) for k in range(NY - 1)]
    for copy in shares:
        copy.start()
    for copy in shares:
        copy.wait_recv()
    for copy in sends + shares:
        copy.wait_send()


def split(value):
    high = value.astype(BF)
    return high, (value - high.astype(F32)).astype(BF)


def compensate_kernel(
    removed_s, s_ref, l_ref, hkr_ref, slabh_ref, down_ref, slabd_ref, corr_o, pruned_o,
    sx, xy, xyh, xyl, rh, rl, rows, slabc, lanes,
):
    t = lax.axis_index("tensor")
    c = t % 2
    pair = t // 2
    eye = lax.broadcasted_iota(jnp.int32, (REM, REM), 0) == lax.broadcasted_iota(jnp.int32, (REM, REM), 1)
    damp = s_ref[0, :, 256:257].astype(F32) + s_ref[0, :, 257:258].astype(F32)
    sx[:, :256] = s_ref[0, :, :256].astype(F32)
    sx[:, 256:] = s_ref[1, :, :256].astype(F32)
    square = sx[...] + jnp.where(eye, damp, 0.0)
    bound = jnp.max(jnp.sum(jnp.abs(square), axis=0, keepdims=True), axis=1, keepdims=True)
    inverse_bound = 1.0 / bound
    low = 0.5 * inverse_bound
    xy[REM:, :] = square * inverse_bound
    xy[:REM, :] = jnp.where(eye, inverse_bound, 0.0)
    for step in range(STEPS):
        middle = 0.5 * (1.0 + low)
        gain = 1.0 / (middle * middle)
        factor = (jnp.where(eye, 2.0 * middle, 0.0) - xy[REM:, :]) * gain
        high, rest = split(factor)
        rh[...] = high
        rl[...] = rest
        parts = [0, 1] if step < STEPS - 1 else [0]
        for part in parts:
            if step == 0 and part == 0:
                xy[:REM, :] = factor * inverse_bound
                continue
            own = pl.ds(part * REM, REM)
            high, rest = split(xy[own, :])
            xyh[...] = high
            xyl[...] = rest
            xy[own, :] = dot(xyh[...], rh[...]) + (dot(xyh[...], rl[...]) + dot(xyl[...], rh[...]))
        low = low * gain
    high, rest = split(xy[:REM, :] * (2.0 / (1.0 + low)))
    rh[...] = high
    rl[...] = rest
    rows[:WIDTH] = hkr_ref[...]
    rows[WIDTH:] = slabh_ref[...]
    coef = dot(rows[...], rh[...]) + dot(rows[...], rl[...])
    high, rest = split(coef)
    for half in range(2):
        cols = pl.ds(half * 1024, 1024)
        change = dot(high, l_ref[half]) + dot(rest, l_ref[half])
        corr_o[:, cols] = (down_ref[:, cols].astype(F32) - change[:WIDTH]).astype(BF)
        slabc[:, cols] = (slabd_ref[:, cols].astype(F32) - change[WIDTH:]).astype(BF)
    indices = pair_indices(removed_s, pair)
    first = t * WIDTH
    even = (pair * 2 + 1) * WIDTH
    even_kept = WIDTH
    for r in indices:
        even_kept = even_kept - jnp.where(r < even, 1, 0)
    rank = ranks(indices, first, WIDTH, 8)
    goal = jnp.where(rank < 0, -1, rank + c * (even_kept - KEPT))[:1]
    row = lax.broadcasted_iota(jnp.int32, (KEPT, WIDTH), 0)
    pack = jnp.where(row == goal, 1.0, 0.0).astype(BF)
    lane = lax.broadcasted_iota(jnp.int32, (8, 16), 1)
    from_odd = even_kept + lane
    from_even = jnp.where(KEPT + lane < even_kept, lane, -1)
    slab_goal = jnp.where(lane < 8, jnp.where(c == 0, from_odd, from_even), -1)[:1]
    row = lax.broadcasted_iota(jnp.int32, (KEPT, 16), 0)
    slab_pack = jnp.where(row == slab_goal, 1.0, 0.0).astype(BF)
    for half in range(2):
        cols = pl.ds(half * 1024, 1024)
        pruned_o[:, cols] = (dot(pack, corr_o[:, cols]) + dot(slab_pack, slabc[:, cols])).astype(BF)


def mixed_kernel(
    hid_ref, corr_ref, out_ref,
    ptx, prx, own, x2, xa, xb, xtx, xrx, ztx, zrx, fin, frx,
    p_s, p_r, a_s, a_r, x_s, x_r, z_s, z_r, f_s, f_r,
):
    x, z, c, d = place()
    other = 1 - c
    partner = at(x, z, other, d)
    right, left = at((x + 1) % NX, z, c, d), at((x + 3) % NX, z, c, d)
    zdev = [at(x, (z + k) % NZ, c, d) for k in range(1, NZ)]
    greet([partner, right, left] + zdev)
    scale = FF ** (-0.5)
    order = (2, 1, 3, 0)
    mine = pl.ds(pl.multiple_of(c * 1024, 1024), 1024)
    theirs = pl.ds(pl.multiple_of(other * 1024, 1024), 1024)
    pairs = {}
    for k in order:
        ptx[k] = (dot(hid_ref[(x + k) % NX], corr_ref[:, theirs]) * scale).astype(BF)
        pairs[k] = remote(ptx.at[k], prx.at[k], p_s.at[k], p_r.at[k], partner)
        pairs[k].start()
    for k in order:
        own[k] = dot(hid_ref[(x + k) % NX], corr_ref[:, mine]) * scale
    pairs[2].wait_recv()
    x2[...] = (own[2] + prx[2].astype(F32)).astype(BF)
    to_right = remote(x2.at[pl.ds(0, 64)], xa, a_s.at[0], a_r.at[0], right)
    to_left = remote(x2.at[pl.ds(64, 64)], xb, a_s.at[1], a_r.at[1], left)
    to_right.start()
    to_left.start()
    pairs[1].wait_recv()
    own[1] = own[1] + prx[1].astype(F32)
    pairs[3].wait_recv()
    own[3] = own[3] + prx[3].astype(F32)
    xtx[0, 64:] = own[1, 64:].astype(BF)
    xtx[1, :64] = own[3, :64].astype(BF)
    low, high = pl.ds(0, 64), pl.ds(64, 64)
    plain = [
        remote(xtx.at[0, high], xrx.at[0, high], x_s.at[0], x_r.at[0], right),
        remote(xtx.at[1, low], xrx.at[1, low], x_s.at[1], x_r.at[1], left),
    ]
    for copy in plain:
        copy.start()
    to_right.wait_recv()
    xtx[0, :64] = (own[1, :64] + xa[...].astype(F32)).astype(BF)
    to_left.wait_recv()
    xtx[1, 64:] = (own[3, 64:] + xb[...].astype(F32)).astype(BF)
    summed = [
        remote(xtx.at[0, low], xrx.at[0, low], x_s.at[2], x_r.at[2], right),
        remote(xtx.at[1, high], xrx.at[1, high], x_s.at[3], x_r.at[3], left),
    ]
    for copy in summed:
        copy.start()
    pairs[0].wait_recv()
    total = own[0] + prx[0].astype(F32)
    for copy in plain + summed:
        copy.wait_recv()
    own[0] = total + xrx[0].astype(F32) + xrx[1].astype(F32)
    zs = []
    for k in range(1, NZ):
        rows = pl.ds(pl.multiple_of(((z + k) % NZ) * 16, 16), 16)
        ztx[k - 1] = own[0, rows].astype(BF)
        copy = remote(ztx.at[k - 1], zrx.at[k - 1], z_s.at[k - 1], z_r.at[k - 1], zdev[k - 1])
        copy.start()
        zs.append(copy)
    total = own[0, pl.ds(pl.multiple_of(z * 16, 16), 16)]
    for k in range(NZ - 1):
        zs[k].wait_recv()
        total = total + zrx[k].astype(F32)
    fin[0] = total[:8]
    fin[1] = total[8:]
    last = remote(fin.at[other], frx, f_s.at[0], f_r.at[0], partner)
    last.start()
    out_ref[:, mine] = fin[c].astype(BF)
    last.wait_recv()
    out_ref[:, theirs] = frx[...].astype(BF)
    for copy in list(pairs.values()) + [to_right, to_left] + plain + summed + zs + [last]:
        copy.wait_send()


def dma(*shape):
    return pltpu.SemaphoreType.DMA(shape)


def vmem():
    return pl.BlockSpec(memory_space=pltpu.VMEM)


def smem():
    return pl.BlockSpec(memory_space=pltpu.SMEM)


def params(collective):
    return pltpu.CompilerParams(
        collective_id=collective, has_side_effects=True, vmem_limit_bytes=VMEM_LIMIT
    )


def out(*shape):
    return jax.ShapeDtypeStruct(shape, BF)


def shards(tokens, gate_weight, up_weight, down_weight, inverse_hessian, damping, removed):
    t = lax.axis_index("tensor")
    d = lax.axis_index("dp")
    own_damp = lax.dynamic_slice(damping, (t * WIDTH + d * BLOCK,), (BLOCK,)).reshape(1, BLOCK)
    tok_all, l_all, s_all, hkr, slab_down, slab_h = pl.pallas_call(
        spread_kernel,
        out_shape=(
            out(2, NX, NZ, 16, 1024), out(2, NX, NZ, 16, 1024), out(2, NX, NZ, 16, 384),
            out(NY, BLOCK, REM), out(16, 2048), out(16, REM),
        ),
        in_specs=[smem(), vmem(), vmem(), vmem(), vmem(), pl.BlockSpec(memory_space=pl.ANY)],
        out_specs=tuple(vmem() for _ in range(6)),
        scratch_shapes=[
            pltpu.VMEM((4, BLOCK, FF // 4), BF),
            pltpu.VMEM((2, 16, 1024), BF), pltpu.VMEM((2, 16, 1024), BF), pltpu.VMEM((2, 16, 384), BF),
            pltpu.VMEM((16, 1024), BF), pltpu.VMEM((16, 1024), BF), pltpu.VMEM((7, 16, 384), BF),
            pltpu.VMEM((16, 2048), BF), pltpu.VMEM((16, REM), BF),
            dma(4), dma(2), dma(2), dma(7), dma(7), dma(3), dma(3), dma(3, 7), dma(3, 7),
            dma(3, 4), dma(3, 4), dma(3, 4), dma(3, 4), dma(2), dma(2),
        ],
        compiler_params=params(1),
        name="spread",
    )(removed, tokens, down_weight, own_damp, removed.reshape(1, REM), inverse_hessian)
    hidden = pl.pallas_call(
        hidden_kernel,
        out_shape=out(NY, 128, WIDTH),
        in_specs=[smem(), vmem(), vmem(), vmem()],
        out_specs=vmem(),
        scratch_shapes=[
            pltpu.VMEM((3, 2, 128, WIDTH), BF), pltpu.VMEM((3, 2, 128, WIDTH), BF),
            pltpu.VMEM((2, 128, WIDTH), F32), dma(3), dma(3), dma(3), dma(3),
        ],
        compiler_params=params(2),
        name="hidden",
    )(removed, tok_all.reshape(2, NY, 128, 1024), gate_weight, up_weight)
    corrected, pruned = pl.pallas_call(
        compensate_kernel,
        out_shape=(out(WIDTH, 2048), out(KEPT, 2048)),
        in_specs=[smem()] + [vmem()] * 6,
        out_specs=(vmem(), vmem()),
        scratch_shapes=[
            pltpu.VMEM((REM, REM), F32), pltpu.VMEM((2 * REM, REM), F32),
            pltpu.VMEM((REM, REM), BF), pltpu.VMEM((REM, REM), BF),
            pltpu.VMEM((REM, REM), BF), pltpu.VMEM((REM, REM), BF),
            pltpu.VMEM((WIDTH + 16, REM), BF), pltpu.VMEM((16, 2048), BF), pltpu.VMEM((8, 128), F32),
        ],
        compiler_params=pltpu.CompilerParams(vmem_limit_bytes=VMEM_LIMIT),
        name="compensate",
    )(
        removed, s_all.reshape(2, REM, 384), l_all.reshape(2, REM, 1024), hkr.reshape(WIDTH, REM), slab_h,
        down_weight, slab_down,
    )
    mixed = pl.pallas_call(
        mixed_kernel,
        out_shape=out(8, 2048),
        in_specs=[vmem(), vmem()],
        out_specs=vmem(),
        scratch_shapes=[
            pltpu.VMEM((4, 128, 1024), BF), pltpu.VMEM((4, 128, 1024), BF), pltpu.VMEM((4, 128, 1024), F32),
            pltpu.VMEM((128, 1024), BF), pltpu.VMEM((64, 1024), BF), pltpu.VMEM((64, 1024), BF),
            pltpu.VMEM((2, 128, 1024), BF), pltpu.VMEM((2, 128, 1024), BF),
            pltpu.VMEM((7, 16, 1024), BF), pltpu.VMEM((7, 16, 1024), BF),
            pltpu.VMEM((2, 8, 1024), F32), pltpu.VMEM((8, 1024), F32),
            dma(4), dma(4), dma(2), dma(2), dma(4), dma(4), dma(7), dma(7), dma(1), dma(1),
        ],
        compiler_params=params(3),
        name="mixed",
    )(hidden, corrected)
    return pruned, mixed


def solution(mesh):
    in_specs = (
        P("tensor", "dp"),
        P("dp", "tensor"),
        P("dp", "tensor"),
        P("tensor", "dp"),
        P(("tensor", "dp"), None),
        P(),
        P(),
    )
    out_specs = (P("tensor", "dp"), P("tensor", "dp"))
    return jax.shard_map(shards, mesh=mesh, in_specs=in_specs, out_specs=out_specs, check_vma=False)
```

time: 601 us -> 136 us (0.23)
  the two profiles are of different devices: /device:TPU:8 before, /device:TPU:1 now
where the time goes in v1:
time: 136 us
  Pallas kernels  127 us (93%)
  local copies, waits for them, and re-layouts  7.82 us (6%)
    pallas_call x1, Pallas kernels, shards(): pl.pallas_call(spread_kernel, out_shape=(out(2, NX, NZ, 16, 1024), out(2,...  49.6 us
    pallas_call x1, Pallas kernels, shards(): pl.pallas_call(hidden_kernel, out_shape=out(NY, 128, WIDTH), in_specs=[sm...  29 us
    pallas_call x1, Pallas kernels, shards(): pl.pallas_call(mixed_kernel, out_shape=out(8, 2048), in_specs=[vmem(), vm...  28.3 us
    pallas_call x1, Pallas kernels, shards(): pl.pallas_call(compensate_kernel, out_shape=(out(WIDTH, 2048), out(KEPT,...  20.2 us
    unnamed x15, local copies, waits for them, and re-layouts  7.74 us

profile of v1, /device:TPU:1, one launch (start us, length us, event | category | flops | bytes accessed | tf_op | source)
XLA Modules:
  0.0 135.5 jit_solution(14416715202959468307)
XLA Ops:
  0.6 0.0 copy-start
  0.7 0.9 copy-done
  1.5 0.1 dynamic-slice_bitcast_fusion.damp_ref
  1.6 0.0 copy-start.1
  1.6 0.7 copy-done.1
  2.3 0.0 copy-start.3
  2.3 0.8 copy-done.3
  3.0 49.6 %spread.1 = (bf16[2,4,8,16,1024]{4,3,2,1,0:T(8,128)(2,1)}, bf16[2,4,8,16,1024]{4,3,2,1,0:T(8,128)(2,1)}, bf16[2,4,8,16,384]{4,3,2,1,0:T(8,128)(2,1)S(1)}, bf16[4...) custom-call(s32[512]{0:T(512)S(1)} %copy-done.1, ...), custom_call_target="tpu_custom_call" | custom-call | tf_op jit(solution)/shard_map/spread/pallas_call | solution.py:483
  52.6 0.0 copy-start.4
  52.6 20.2 %compensate.1 = (bf16[416,2048]{1,0:T(8,128)(2,1)}, bf16[408,2048]{1,0:T(8,128)(2,1)}) custom-call(s32[512]{0:T(512)S(1)} %copy-done.1, bf16[2,512,384]{2,1,0:T(8,128)(2,1)S(1)} %bitcast.7, bf16[2,512,1024]{2,1,0:T(8,128)(2,1)} %bitcast.11, bf16[416,512]{1,0:T(8,128)(2,1)S(1)} %bitcast.8, bf16[16,512]{1,0:T(8,128)(2,1)S(1)} %get-tuple-element.13.slabh_ref, ...), custom_call_target="tpu_custom_call" | custom-call | tf_op jit(solution)/shard_map/compensate/pallas_call | solution.py:514
  72.8 0.0 copy-start.5
  72.8 0.0 copy-done.4
  72.8 2.4 %copy.10.up_ref = bf16[2048,416]{1,0:T(8,128)(2,1)} copy(bf16[2048,416]{0,1:T(8,128)(2,1)S(1)} %copy-done.4) | data formatting | bytes 3407872 | tf_op args[2]
  75.2 0.0 copy-done.5
  75.2 0.0 copy-start.2
  75.3 2.4 %copy.9.gate_ref = bf16[2048,416]{1,0:T(8,128)(2,1)} copy(bf16[2048,416]{0,1:T(8,128)(2,1)S(1)} %copy-done.5) | data formatting | bytes 3407872 | tf_op args[1]
  77.6 0.0 copy-done.2
  77.6 29.0 %hidden.1.hid_ref = bf16[4,128,416]{2,1,0:T(8,128)(2,1)S(1)} custom-call(s32[512]{0:T(512)S(1)} %copy-done.2, bf16[2,4,128,1024]{3,2,1,0:T(8,128)(2,1)} %bitcast.10, bf16[2048,416]{1,0:T(8,128)(2,1)} %copy.9.gate_ref, bf16[2048,416]{1,0:T(8,128)(2,1)} %copy.10.up_ref), custom_call_target="tpu_custom_call" | custom-call | tf_op jit(solution)/shard_map/hidden/pallas_call | solution.py:502
  106.6 28.3 %mixed.1 = bf16[8,2048]{1,0:T(8,128)(2,1)S(1)} custom-call(bf16[4,128,416]{2,1,0:T(8,128)(2,1)S(1)} %hidden.1.hid_ref, bf16[416,2048]{1,0:T(8,128)(2,1)} %get-tuple-element.17.corr_ref), custom_call_target="tpu_custom_call" | custom-call | tf_op jit(solution)/shard_map/mixed/pallas_call | solution.py:531
  134.9 0.6 copy.12
Async XLA Ops:
  0.6 0.9 copy-start
  1.6 0.7 copy-start.1
  2.3 0.8 copy-start.3
  52.6 20.2 %copy-start.4 = (bf16[2048,416]{0,1:T(8,128)(2,1)S(1)}, bf16[2048,416]{0,1:T(8,128)(2,1)}, u32[]{:S(2)}) copy-start(bf16[2048,416]{0,1:T(8,128)(2,1)} %param.9) | copy-start | bytes 5111812
  72.8 2.4 %copy-start.5 = (bf16[2048,416]{0,1:T(8,128)(2,1)S(1)}, bf16[2048,416]{0,1:T(8,128)(2,1)}, u32[]{:S(2)}) copy-start(bf16[2048,416]{0,1:T(8,128)(2,1)} %param.8) | copy-start | bytes 5111812
  75.2 2.4 %copy-start.2 = (s32[512]{0:T(512)S(1)}, s32[512]{0:T(512)}, u32[]{:S(2)}) copy-start(s32[512]{0:T(512)} %removed_s.5) | copy-start | bytes 6148

commit v2 on v0

v2 whole, which is shorter than its diff:
```python
import jax
import jax.numpy as jnp
from jax import lax
from jax.experimental import pallas as pl
from jax.experimental.pallas import tpu as pltpu
from jax.sharding import PartitionSpec as P

MESH = pl.DeviceIdType.MESH
BF = jnp.bfloat16
F32 = jnp.float32
NX, NZ, NY = 4, 8, 4
WIDTH = 416
BLOCK = 104
KEPT = 408
FF = 26624
REM = 512
STEPS = 8
HALF = REM // 2
VMEM_LIMIT = 56 * 1024 * 1024


def dot(a, b):
    return jnp.dot(a, b, preferred_element_type=F32)


def place():
    t = lax.axis_index("tensor")
    d = lax.axis_index("dp")
    return t // 16, (t // 2) % 8, t % 2, d


def at(x, z, c, d):
    return (x * 16 + z * 2 + c, d)


def remote(src, dst, send, recv, device):
    return pltpu.make_async_remote_copy(
        src_ref=src, dst_ref=dst, send_sem=send, recv_sem=recv, device_id=device, device_id_type=MESH
    )


def greet(devices):
    barrier = pltpu.get_barrier_semaphore()
    for device in devices:
        pl.semaphore_signal(barrier, inc=1, device_id=device, device_id_type=MESH)
    pl.semaphore_wait(barrier, len(devices))


def pair_indices(removed_s, pair):
    return [removed_s[pair * 16 + j] for j in range(16)]


def index_rows(indices, lanes):
    row = lax.broadcasted_iota(jnp.int32, (16, lanes), 0)
    out = jnp.full((16, lanes), -1, jnp.int32)
    for j, r in enumerate(indices):
        out = jnp.where(row == j, r, out)
    return out


def dot_nt(a, b):
    return lax.dot_general(a, b, (((1,), (1,)), ((), ())), preferred_element_type=F32)


def ranks(indices, first, offset, lanes, rows=16):
    lane = lax.broadcasted_iota(jnp.int32, (rows, lanes), 1) + (first + offset)
    below = jnp.zeros((rows, lanes), jnp.int32)
    gone = jnp.zeros((rows, lanes), jnp.int32)
    for r in indices:
        mine = jnp.where(r >= first, 1, 0)
        below = below + jnp.where(r < lane, mine, 0)
        gone = gone + jnp.where(r == lane, 1, 0)
    return jnp.where(gone > 0, -1, lane - first - below)


def split(value):
    high = value.astype(BF)
    return high, (value - high.astype(F32)).astype(BF)


def dot2(pair, b):
    return dot(pair[0], b) + dot(pair[1], b)


def dot3(a, b):
    return dot(a[0], b[0]) + (dot(a[0], b[1]) + dot(a[1], b[0]))


def newton(xy, between):
    n = HALF
    eye = lax.broadcasted_iota(jnp.int32, (n, n), 0) == lax.broadcasted_iota(jnp.int32, (n, n), 1)
    square = xy[n:, :]
    bound = jnp.max(jnp.sum(jnp.abs(square), axis=0, keepdims=True), axis=1, keepdims=True)
    inverse_bound = 1.0 / bound
    low = 0.5 * inverse_bound
    xy[n:, :] = square * inverse_bound
    for step in range(STEPS):
        middle = 0.5 * (1.0 + low)
        gain = 1.0 / (middle * middle)
        factor = (jnp.where(eye, 2.0 * middle, 0.0) - xy[n:, :]) * gain
        right = split(factor)
        if step == 0:
            xy[n:, :] = dot3(split(xy[n:, :]), right)
            xy[:n, :] = factor * inverse_bound
        elif step < STEPS - 1:
            xy[...] = dot3(split(xy[...]), right)
        else:
            xy[:n, :] = dot3(split(xy[:n, :]), right)
        low = low * gain
        between(step)
    xy[:n, :] = xy[:n, :] * (2.0 / (1.0 + low))


def prune_kernel(
    removed_s, tok_h, gate_h, up_h, down_h, hess_h, damp_h, removed_h,
    pruned_o, mixed_o,
    tok_in, down, damp, removed_v, hbuf, weight,
    tok_o, l_o, s_o, hkr_o, slabd_o, slabh_o,
    lpad, spad, l_rx, s_rx, slabd_tx, slabh_tx,
    lhs, pre, pre_tx, pre_rx, pre_own, hid,
    xy, inv, rows, corr, slabc,
    ptx, prx, own, x2, xa, xb, xtx, xrx, ztx, zrx, fin, frx,
    load_s, hess_s, pair_s, pair_r, sc_s, sc_r, y_s, y_r, z_s, z_r, x_s, x_r, c_s, c_r, sl_s, sl_r,
    ps_s, ps_r, h_s, h_r,
    p_s, p_r, a_s, a_r, e_s, e_r, w_s, w_r, f_s, f_r,
):
    x, z, c, d = place()
    other = 1 - c
    pair = x * NZ + z
    first = (pair * 2 + c) * WIDTH
    quarter = FF // 4

    def load(src, dst, sem):
        copy = pltpu.make_async_copy(src, dst, sem)
        copy.start()
        return copy

    tok_load = load(tok_h, tok_in, load_s.at[0])
    removed_load = load(removed_h, removed_v, load_s.at[1])
    damp_load = load(damp_h, damp, load_s.at[2])
    hess_loads = [load(hess_h.at[:, pl.ds(g * quarter, quarter)], hbuf.at[g], hess_s.at[g]) for g in range(4)]
    down_load = load(down_h, down, load_s.at[3])
    gate_load = load(gate_h, weight.at[pl.ds(0, WIDTH)], load_s.at[4])
    up_load = load(up_h, weight.at[pl.ds(WIDTH, WIDTH)], load_s.at[5])

    partner = at(x, z, other, d)
    right, left = at((x + 1) % NX, z, c, d), at((x + 3) % NX, z, c, d)
    ydev = [at(x, z, c, (d + k) % NY) for k in range(1, NY)]
    ycross = [at(x, z, other, (d + k) % NY) for k in range(1, NY)]
    zdev = [at(x, (z + k) % NZ, c, d) for k in range(1, NZ)]
    greet([partner, right, left] + ydev + ycross + zdev)
    pending = []

    def send(src, dst, s, r, device):
        copy = remote(src, dst, s, r, device)
        copy.start()
        pending.append(copy)
        return copy

    def arrived(copies):
        for copy in copies:
            copy.wait_recv()

    def z_sends(array, n):
        here = array.at[c, x, z]
        return [send(here, here, z_s.at[n, k], z_r.at[n, k], zdev[k]) for k in range(NZ - 1)]

    def x_sends(array, n):
        here = array.at[c, x]
        return [
            send(here, here, x_s.at[n, 0], x_r.at[n, 0], right),
            send(here, here, x_s.at[n, 1], x_r.at[n, 1], left),
        ]

    def x_forwards(array, n):
        low = array.at[c, (x + 3) % NX, pl.ds(0, 4)]
        high = array.at[c, (x + 1) % NX, pl.ds(4, 4)]
        return [
            send(low, low, x_s.at[n, 2], x_r.at[n, 2], right),
            send(high, high, x_s.at[n, 3], x_r.at[n, 3], left),
        ]

    def core_send(array, n, k):
        here = array.at[c, (x + k) % NX]
        return send(here, here, c_s.at[n, k], c_r.at[n, k], partner)

    tok_load.wait()
    tok = tok_in[...].astype(F32)
    tok_o[c, x, z] = jnp.concatenate([tok[:, :1024], tok[:, 1024:]], axis=0).astype(BF)
    tok_z = z_sends(tok_o, 0)

    indices = pair_indices(removed_s, pair)
    removed_load.wait()
    chunk = quarter // 4
    for g in range(4):
        hess_loads[g].wait()
        wanted = removed_v[g : g + 1, :]
        total = jnp.zeros((BLOCK, 128), F32)
        for q in range(4):
            start = g * quarter + q * chunk
            channel = lax.broadcasted_iota(jnp.int32, (chunk, 128), 0) + start
            hot = jnp.where(channel == wanted, 1.0, 0.0).astype(BF)
            total = total + dot(hbuf[g, :, q * chunk : (q + 1) * chunk], hot)
        hkr_o[d, :, g * 128 : (g + 1) * 128] = total.astype(BF)
    rows104 = index_rows(indices, BLOCK)
    lane104 = lax.broadcasted_iota(jnp.int32, (16, BLOCK), 1)
    block_first = first + d * BLOCK
    pick104 = jnp.where(lane104 + block_first == rows104, 1.0, 0.0)
    own_rows = dot(pick104.astype(BF), hkr_o[d]).astype(BF)
    damp_load.wait()
    lane128 = lax.broadcasted_iota(jnp.int32, (16, 128), 1)
    row128 = lax.broadcasted_iota(jnp.int32, (16, 128), 0)
    found = jnp.zeros((16, 128), F32)
    for j, r in enumerate(indices):
        line = damp[pl.ds(r // 128, 1), :]
        here = jnp.where(r >= block_first, jnp.where(r < block_first + BLOCK, j, -1), -1)
        found = jnp.where(row128 == here, jnp.where(lane128 == r % 128, line, 0.0), found)
    damped = jnp.sum(found, axis=1, keepdims=True)
    high = damped.astype(BF).astype(F32)
    extra = jnp.where(lane128 == 0, high, jnp.where(lane128 == 1, damped - high, 0.0)).astype(BF)
    for half in range(2):
        spad[half, :, :256] = own_rows[:, half * 256 : (half + 1) * 256]
        spad[half, :, 256:] = extra
    s_sends = []
    for k in range(NY - 1):
        s_sends.append(send(spad.at[c], s_rx.at[k], sc_s.at[k], sc_r.at[k], ydev[k]))
        s_sends.append(send(spad.at[other], s_rx.at[3 + k], sc_s.at[3 + k], sc_r.at[3 + k], ycross[k]))
    s_sends.append(send(spad.at[other], s_rx.at[6], sc_s.at[6], sc_r.at[6], partner))
    h_sends = [send(hkr_o.at[d], hkr_o.at[d], y_s.at[k], y_r.at[k], ydev[k]) for k in range(NY - 1)]

    down_load.wait()
    rows416 = index_rows(indices, WIDTH)
    lane416 = lax.broadcasted_iota(jnp.int32, (16, WIDTH), 1)
    pick = jnp.where(lane416 + first == rows416, 1.0, 0.0).astype(BF)
    lost = dot(pick, down[...]).astype(BF)
    lpad[0] = lost[:, :1024]
    lpad[1] = lost[:, 1024:]
    l_pair = send(lpad.at[other], l_rx, pair_s.at[0], pair_r.at[0], partner)
    row16 = lax.broadcasted_iota(jnp.int32, (16, WIDTH), 0)
    target = jnp.where(row16 < 8, row16 + (1 - c) * KEPT, -7)
    slab_pick = jnp.where(ranks(indices, first, 0, WIDTH) == target, 1.0, 0.0)
    slabd_tx[...] = dot(slab_pick.astype(BF), down[...]).astype(BF)
    slabd = send(slabd_tx, slabd_o, sl_s.at[0], sl_r.at[0], partner)

    arrived(tok_z)
    tok_x = x_sends(tok_o, 0)
    tok_c = {0: core_send(tok_o, 0, 0)}
    arrived(s_sends)
    total = spad[c].astype(F32)
    for k in range(7):
        total = total + s_rx[k].astype(F32)
    s_o[c, x, z] = total.astype(BF)
    s_z = z_sends(s_o, 2)

    partials = {}

    def preact(k):
        arrived([tok_c[k]])
        b = (x + k) % NX
        for core in range(2):
            value = tok_o[core, b].astype(F32)
            lhs[0, core * 64 : core * 64 + 64] = value[:, :8].reshape(64, 1024).astype(BF)
            lhs[1, core * 64 : core * 64 + 64] = value[:, 8:].reshape(64, 1024).astype(BF)
        pre[...] = dot_nt(lhs[0], weight[:, :1024]) + dot_nt(lhs[1], weight[:, 1024:])
        sends = []
        for m in range(NY - 1):
            part = pl.ds(pl.multiple_of(((d + 1 + m) % NY) * 32, 32), 32)
            pre_tx[k, m] = pre[part, :].astype(BF)
            sends.append(send(pre_tx.at[k, m], pre_rx.at[k, m], ps_s.at[k, m], ps_r.at[k, m], ydev[m]))
        pre_own[k] = pre[pl.ds(pl.multiple_of(d * 32, 32), 32), :]
        partials[k] = sends

    shares = {}

    def gated(k):
        arrived(partials[k])
        value = pre_own[k]
        for m in range(NY - 1):
            value = value + pre_rx[k, m].astype(F32)
        gate, up = value[:, :WIDTH], value[:, WIDTH:]
        lane = lax.broadcasted_iota(jnp.int32, (32, WIDTH), 1) + first
        hidden = gate / (1.0 + jnp.exp(-gate)) * up
        for r in indices:
            hidden = jnp.where(lane == r, 0.0, hidden)
        hid[k, d] = hidden.astype(BF)
        here = hid.at[k, d]
        shares[k] = [send(here, here, h_s.at[k, m], h_r.at[k, m], ydev[m]) for m in range(NY - 1)]

    gate_load.wait()
    up_load.wait()
    preact(0)
    arrived(s_z)
    s_x = x_sends(s_o, 2)
    s_c = [core_send(s_o, 2, 0)]
    arrived(tok_x)
    tok_f = x_forwards(tok_o, 0)
    tok_c[1] = core_send(tok_o, 0, 1)
    tok_c[3] = core_send(tok_o, 0, 3)
    arrived(s_x)
    s_f = x_forwards(s_o, 2)
    s_c += [core_send(s_o, 2, 1), core_send(s_o, 2, 3)]
    preact(1)
    preact(3)
    arrived(s_f)
    s_c.append(core_send(s_o, 2, 2))
    arrived([l_pair])
    l_o[c, x, z] = lpad[c] + l_rx[...]
    l_z = z_sends(l_o, 1)
    arrived(tok_f)
    tok_c[2] = core_send(tok_o, 0, 2)
    arrived(s_c)

    later = {}

    def lost_x():
        arrived(l_z)
        later["x"] = x_sends(l_o, 1)
        later["c"] = [core_send(l_o, 1, 0)]

    def lost_forward():
        arrived(later["x"])
        later["f"] = x_forwards(l_o, 1)
        later["c"] += [core_send(l_o, 1, 1), core_send(l_o, 1, 3)]

    def lost_last():
        arrived(later["f"])
        later["c"].append(core_send(l_o, 1, 2))

    def gather_rows():
        arrived(h_sends)
        slab = jnp.zeros((16, REM), F32)
        for k in range(NY):
            mine = ranks(indices, first, k * BLOCK, BLOCK) == target[:, :BLOCK]
            slab = slab + dot(jnp.where(mine, 1.0, 0.0).astype(BF), hkr_o[k])
            rows[k * BLOCK : (k + 1) * BLOCK] = hkr_o[k].astype(F32)
        slabh_tx[...] = slab.astype(BF)
        later["s"] = send(slabh_tx, slabh_o, sl_s.at[1], sl_r.at[1], partner)

    eye = lax.broadcasted_iota(jnp.int32, (HALF, HALF), 0) == lax.broadcasted_iota(jnp.int32, (HALF, HALF), 1)

    def s_block(i, j):
        return s_o[j, 2 * i : 2 * i + 2, :, :, :256].reshape(HALF, 256)

    def diagonal(i):
        damping = s_o[0, 2 * i : 2 * i + 2, :, :, 256:].reshape(HALF, 128).astype(F32)
        return jnp.where(eye, damping[:, 0:1] + damping[:, 1:2], 0.0)

    xy[HALF:, :] = s_block(0, 0).astype(F32) + diagonal(0)
    tasks = {
        0: [lambda: preact(2)], 1: [lost_x], 2: [lambda: gated(0)], 4: [lambda: gated(1), lambda: gated(3)],
        5: [lost_forward], 7: [lambda: gated(2), gather_rows],
    }

    def first_tasks(step):
        for task in tasks.get(step, []):
            task()

    newton(xy, first_tasks)
    inv[...] = xy[:HALF, :]
    a_inv = split(inv[...])
    b_block = s_block(0, 1)
    v = dot(s_block(1, 0), a_inv[0]) + dot(s_block(1, 0), a_inv[1])
    xy[HALF:, :] = s_block(1, 1).astype(F32) + diagonal(1) - dot2(split(v), b_block)
    newton(xy, lambda step: lost_last() if step == 1 else None)
    e_inv = split(xy[:HALF, :])
    arrived([slabd, later["s"]])
    rows[WIDTH:] = slabh_o[...].astype(F32)
    q = dot(rows[:, :HALF].astype(BF), a_inv[0]) + dot(rows[:, :HALF].astype(BF), a_inv[1])
    u = rows[:, HALF:] - dot2(split(q), b_block)
    second = dot3(split(u), e_inv)
    pair_first = split(q - dot3(split(second), split(v)))
    pair_second = split(second)
    arrived(later["c"])
    lost_all = [l_o[h].reshape(REM, 1024) for h in range(2)]
    for half in range(2):
        cols = pl.ds(half * 1024, 1024)
        change = dot2(pair_first, lost_all[half][:HALF]) + dot2(pair_second, lost_all[half][HALF:])
        corr[:, cols] = (down[:, cols].astype(F32) - change[:WIDTH]).astype(BF)
        slabc[:, cols] = (slabd_o[:, cols].astype(F32) - change[WIDTH:]).astype(BF)

    scale = FF ** (-0.5)
    order = (2, 1, 3, 0)
    mine = pl.ds(pl.multiple_of(c * 1024, 1024), 1024)
    theirs = pl.ds(pl.multiple_of(other * 1024, 1024), 1024)
    pairs = {}
    for k in order:
        arrived(shares[k])
        ptx[k] = (dot(hid[k].reshape(128, WIDTH), corr[:, theirs]) * scale).astype(BF)
        pairs[k] = send(ptx.at[k], prx.at[k], p_s.at[k], p_r.at[k], partner)
    for k in order:
        own[k] = dot(hid[k].reshape(128, WIDTH), corr[:, mine]) * scale
    arrived([pairs[2]])
    x2[...] = (own[2] + prx[2].astype(F32)).astype(BF)
    low, top = pl.ds(0, 64), pl.ds(64, 64)
    to_right = send(x2.at[low], xa, a_s.at[0], a_r.at[0], right)
    to_left = send(x2.at[top], xb, a_s.at[1], a_r.at[1], left)
    arrived([pairs[1]])
    own[1] = own[1] + prx[1].astype(F32)
    xtx[0, 64:] = own[1, 64:].astype(BF)
    plain = [send(xtx.at[0, top], xrx.at[0, top], e_s.at[0], e_r.at[0], right)]
    arrived([pairs[3]])
    own[3] = own[3] + prx[3].astype(F32)
    xtx[1, :64] = own[3, :64].astype(BF)
    plain.append(send(xtx.at[1, low], xrx.at[1, low], e_s.at[1], e_r.at[1], left))

    even = (pair * 2 + 1) * WIDTH
    even_kept = WIDTH
    for r in indices:
        even_kept = even_kept - jnp.where(r < even, 1, 0)
    rank = ranks(indices, first, 0, WIDTH, 8)
    goal = jnp.where(rank < 0, -1, rank + c * (even_kept - KEPT))[:1]
    row = lax.broadcasted_iota(jnp.int32, (KEPT, WIDTH), 0)
    pack = jnp.where(row == goal, 1.0, 0.0).astype(BF)
    lane = lax.broadcasted_iota(jnp.int32, (8, 16), 1)
    from_odd = even_kept + lane
    from_even = jnp.where(KEPT + lane < even_kept, lane, -1)
    slab_goal = jnp.where(lane < 8, jnp.where(c == 0, from_odd, from_even), -1)[:1]
    row = lax.broadcasted_iota(jnp.int32, (KEPT, 16), 0)
    slab_pack = jnp.where(row == slab_goal, 1.0, 0.0).astype(BF)

    def packed(half):
        cols = pl.ds(half * 1024, 1024)
        pruned_o[:, cols] = (dot(pack, corr[:, cols]) + dot(slab_pack, slabc[:, cols])).astype(BF)

    packed(0)
    arrived([to_right])
    xtx[0, :64] = (own[1, :64] + xa[...].astype(F32)).astype(BF)
    summed = [send(xtx.at[0, low], xrx.at[0, low], e_s.at[2], e_r.at[2], right)]
    arrived([to_left])
    xtx[1, 64:] = (own[3, 64:] + xb[...].astype(F32)).astype(BF)
    summed.append(send(xtx.at[1, top], xrx.at[1, top], e_s.at[3], e_r.at[3], left))
    packed(1)
    arrived([pairs[0]])
    total = own[0] + prx[0].astype(F32)
    arrived(plain + summed)
    own[0] = total + xrx[0].astype(F32) + xrx[1].astype(F32)

    def z_rows(k):
        start = pl.multiple_of(((z + k) % NZ) * 8, 8)
        return jnp.concatenate([own[0, pl.ds(start, 8)], own[0, pl.ds(64 + start, 8)]], axis=0)

    zs = []
    for k in range(1, NZ):
        ztx[k - 1] = z_rows(k).astype(BF)
        zs.append(send(ztx.at[k - 1], zrx.at[k - 1], w_s.at[k - 1], w_r.at[k - 1], zdev[k - 1]))
    total = z_rows(0)
    for k in range(NZ - 1):
        arrived([zs[k]])
        total = total + zrx[k].astype(F32)
    fin[0] = total[:8]
    fin[1] = total[8:]
    last = send(fin.at[other], frx, f_s.at[0], f_r.at[0], partner)
    mixed_o[:, mine] = fin[c].astype(BF)
    arrived([last])
    mixed_o[:, theirs] = frx[...].astype(BF)
    for copy in pending:
        copy.wait_send()


def dma(*shape):
    return pltpu.SemaphoreType.DMA(shape)


def vmem():
    return pl.BlockSpec(memory_space=pltpu.VMEM)


def hbm():
    return pl.BlockSpec(memory_space=pl.ANY)


def out(*shape):
    return jax.ShapeDtypeStruct(shape, BF)


def shards(tokens, gate_weight, up_weight, down_weight, inverse_hessian, damping, removed):
    def bf(*shape):
        return pltpu.VMEM(shape, BF)

    def f32(*shape):
        return pltpu.VMEM(shape, F32)

    return pl.pallas_call(
        prune_kernel,
        out_shape=(out(KEPT, 2048), out(8, 2048)),
        in_specs=[pl.BlockSpec(memory_space=pltpu.SMEM)] + [hbm()] * 7,
        out_specs=(vmem(), vmem()),
        scratch_shapes=[
            bf(8, 2048), bf(WIDTH, 2048), f32(FF // 128, 128), pltpu.VMEM((4, 128), jnp.int32),
            bf(4, BLOCK, FF // 4), bf(2 * WIDTH, 2048),
            bf(2, NX, NZ, 16, 1024), bf(2, NX, NZ, 16, 1024), bf(2, NX, NZ, 16, 384),
            bf(NY, BLOCK, REM), bf(16, 2048), bf(16, REM),
            bf(2, 16, 1024), bf(2, 16, 384), bf(16, 1024), bf(7, 16, 384), bf(16, 2048), bf(16, REM),
            bf(2, 128, 1024), f32(128, 2 * WIDTH), bf(4, 3, 32, 2 * WIDTH), bf(4, 3, 32, 2 * WIDTH),
            f32(4, 32, 2 * WIDTH), bf(4, NY, 32, WIDTH),
            f32(2 * HALF, HALF), f32(HALF, HALF), f32(WIDTH + 16, REM), bf(WIDTH, 2048), bf(16, 2048),
            bf(4, 128, 1024), bf(4, 128, 1024), f32(4, 128, 1024), bf(128, 1024), bf(64, 1024), bf(64, 1024),
            bf(2, 128, 1024), bf(2, 128, 1024), bf(7, 16, 1024), bf(7, 16, 1024), f32(2, 8, 1024), f32(8, 1024),
            dma(6), dma(4), dma(1), dma(1), dma(7), dma(7), dma(3), dma(3), dma(3, 7), dma(3, 7),
            dma(3, 4), dma(3, 4), dma(3, 4), dma(3, 4), dma(2), dma(2),
            dma(4, 3), dma(4, 3), dma(4, 3), dma(4, 3),
            dma(4), dma(4), dma(2), dma(2), dma(4), dma(4), dma(7), dma(7), dma(1), dma(1),
        ],
        compiler_params=pltpu.CompilerParams(
            collective_id=1, has_side_effects=True, vmem_limit_bytes=VMEM_LIMIT
        ),
        name="prune",
    )(
        removed, tokens, gate_weight.T, up_weight.T, down_weight, inverse_hessian,
        damping.reshape(FF // 128, 128), removed.reshape(4, 128),
    )


def solution(mesh):
    in_specs = (
        P("tensor", "dp"),
        P("dp", "tensor"),
        P("dp", "tensor"),
        P("tensor", "dp"),
        P(("tensor", "dp"), None),
        P(),
        P(),
    )
    out_specs = (P("tensor", "dp"), P("tensor", "dp"))
    return jax.shard_map(shards, mesh=mesh, in_specs=in_specs, out_specs=out_specs, check_vma=False)
```

time: 601 us -> 90.9 us (0.15)
  the two profiles are of different devices: /device:TPU:8 before, /device:TPU:1 now
where the time goes in v2:
time: 90.9 us; the launch traced here: 89.9 us
  Pallas kernels  85.8 us (94%)
  local copies, waits for them, and re-layouts  3.44 us (4%)
    pallas_call x1, Pallas kernels, shards(): pl.pallas_call(prune_kernel, out_shape=(out(KEPT, 2048), out(8, 2048)), i...  85.8 us
    unnamed x4, local copies, waits for them, and re-layouts  3.44 us

profile of v2, /device:TPU:1, one launch (start us, length us, event | category | flops | bytes accessed | tf_op | source)
XLA Modules:
  0.0 89.9 jit_solution(16919037635699677813)
XLA Ops:
  0.6 85.8 %prune.1 = (bf16[408,2048]{1,0:T(8,128)(2,1)}, bf16[8,2048]{1,0:T(8,128)(2,1)}) custom-call(s32[512]{0:T(512)} %removed_s.1, bf16[8,2048]{1,0:T(8,128)(2,1)} %tok_h.1, bf16[416,2048]{1,0:T(8,128)(2,1)} %bitcast.4, bf16[416,2048]{1,0:T(8,128)(2,1)} %bitcast.5, bf16[416,2048]{1,0:T(8,128)(2,1)} %down_h.1, bf16[104,26624]{1,0:T(8,128)(2,1)} %hess_h.1, ...), custom_call_target="tpu_custom_call" | custom-call | tf_op jit(solution)/shard_map/prune/pallas_call | solution.py:483
  86.4 0.0 copy-start
  86.4 2.8 %copy.11 = bf16[408,2048]{1,0:T(8,128)(2,1)} copy(bf16[408,2048]{1,0:T(8,128)(2,1)} %get-tuple-element.4) | data formatting | bytes 3342336
  89.3 0.0 copy-done
  89.3 0.6 copy.12
Async XLA Ops:
  86.4 2.8 %copy-start = (bf16[8,2048]{1,0:T(8,128)(2,1)S(1)}, bf16[8,2048]{1,0:T(8,128)(2,1)}, u32[]{:S(2)}) copy-start(bf16[8,2048]{1,0:T(8,128)(2,1)} %get-tuple-element.5) | copy-start | bytes 98308

commit v3 on v2

--- a/solution.py
+++ b/solution.py
@@ -16,6 +16,7 @@
 REM = 512
 STEPS = 8
 HALF = REM // 2
+PIECES = 8
 VMEM_LIMIT = 56 * 1024 * 1024
 
 
@@ -122,7 +123,7 @@
     ptx, prx, own, x2, xa, xb, xtx, xrx, ztx, zrx, fin, frx,
     load_s, hess_s, pair_s, pair_r, sc_s, sc_r, y_s, y_r, z_s, z_r, x_s, x_r, c_s, c_r, sl_s, sl_r,
     ps_s, ps_r, h_s, h_r,
-    p_s, p_r, a_s, a_r, e_s, e_r, w_s, w_r, f_s, f_r,
+    p_s, p_r, a_s, a_r, e_s, e_r, w_s, w_r, f_s, f_r, packed_v, out_s,
 ):
     x, z, c, d = place()
     other = 1 - c
@@ -186,21 +187,24 @@
 
     tok_load.wait()
     tok = tok_in[...].astype(F32)
-    tok_o[c, x, z] = jnp.concatenate([tok[:, :1024], tok[:, 1024:]], axis=0).astype(BF)
-    tok_z = z_sends(tok_o, 0)
+    for h in range(2):
+        cols = slice(h * 512, h * 512 + 512)
+        tok_o[h, c, x, z] = jnp.concatenate([tok[:, :1024][:, cols], tok[:, 1024:][:, cols]], axis=0).astype(BF)
+    tok_z = [z_sends(tok_o.at[h], 2 * h) for h in range(2)]
 
     indices = pair_indices(removed_s, pair)
     removed_load.wait()
     chunk = quarter // 4
+    lane = lax.broadcasted_iota(jnp.int32, (1, 128), 1)
+    channel = lax.broadcasted_iota(jnp.int32, (chunk, 128), 0)
     for g in range(4):
         hess_loads[g].wait()
-        wanted = removed_v[g : g + 1, :]
+        wanted = removed_v[g : g + 1, :] - (g * quarter + (lane // 32) * chunk)
+        hot = jnp.where(channel == wanted, 1.0, 0.0).astype(BF)
         total = jnp.zeros((BLOCK, 128), F32)
         for q in range(4):
-            start = g * quarter + q * chunk
-            channel = lax.broadcasted_iota(jnp.int32, (chunk, 128), 0) + start
-            hot = jnp.where(channel == wanted, 1.0, 0.0).astype(BF)
-            total = total + dot(hbuf[g, :, q * chunk : (q + 1) * chunk], hot)
+            part = dot(hbuf[g, :, q * chunk : (q + 1) * chunk], hot)
+            total = jnp.where(lane // 32 == q, part, total)
         hkr_o[d, :, g * 128 : (g + 1) * 128] = total.astype(BF)
     rows104 = index_rows(indices, BLOCK)
     lane104 = lax.broadcasted_iota(jnp.int32, (16, BLOCK), 1)
@@ -242,25 +246,35 @@
     slabd_tx[...] = dot(slab_pick.astype(BF), down[...]).astype(BF)
     slabd = send(slabd_tx, slabd_o, sl_s.at[0], sl_r.at[0], partner)
 
-    arrived(tok_z)
-    tok_x = x_sends(tok_o, 0)
-    tok_c = {0: core_send(tok_o, 0, 0)}
     arrived(s_sends)
     total = spad[c].astype(F32)
     for k in range(7):
         total = total + s_rx[k].astype(F32)
     s_o[c, x, z] = total.astype(BF)
-    s_z = z_sends(s_o, 2)
+    s_z = z_sends(s_o, 3)
+    arrived([l_pair])
+    l_o[c, x, z] = lpad[c] + l_rx[...]
+    tok_x = []
+    for h in range(2):
+        arrived(tok_z[h])
+        tok_x.append(x_sends(tok_o.at[h], 2 * h))
+    tok_c = {0: [core_send(tok_o.at[h], 2 * h, 0) for h in range(2)]}
+    l_z = z_sends(l_o, 1)
+    arrived(s_z)
+    s_x = x_sends(s_o, 3)
+    s_c = [core_send(s_o, 3, 0)]
 
     partials = {}
 
     def preact(k):
-        arrived([tok_c[k]])
+        arrived(tok_c[k])
         b = (x + k) % NX
         for core in range(2):
-            value = tok_o[core, b].astype(F32)
-            lhs[0, core * 64 : core * 64 + 64] = value[:, :8].reshape(64, 1024).astype(BF)
-            lhs[1, core * 64 : core * 64 + 64] = value[:, 8:].reshape(64, 1024).astype(BF)
+            for h in range(2):
+                value = tok_o[h, core, b].astype(F32)
+                cols = slice(h * 512, h * 512 + 512)
+                lhs[0, core * 64 : core * 64 + 64, cols] = value[:, :8].reshape(64, 512).astype(BF)
+                lhs[1, core * 64 : core * 64 + 64, cols] = value[:, 8:].reshape(64, 512).astype(BF)
         pre[...] = dot_nt(lhs[0], weight[:, :1024]) + dot_nt(lhs[1], weight[:, 1024:])
         sends = []
         for m in range(NY - 1):
@@ -289,33 +303,28 @@
     gate_load.wait()
     up_load.wait()
     preact(0)
-    arrived(s_z)
-    s_x = x_sends(s_o, 2)
-    s_c = [core_send(s_o, 2, 0)]
-    arrived(tok_x)
-    tok_f = x_forwards(tok_o, 0)
-    tok_c[1] = core_send(tok_o, 0, 1)
-    tok_c[3] = core_send(tok_o, 0, 3)
+    tok_f = []
+    tok_c[1], tok_c[3] = [], []
+    for h in range(2):
+        arrived(tok_x[h])
+        tok_f.append(x_forwards(tok_o.at[h], 2 * h))
+        tok_c[1].append(core_send(tok_o.at[h], 2 * h, 1))
+        tok_c[3].append(core_send(tok_o.at[h], 2 * h, 3))
     arrived(s_x)
-    s_f = x_forwards(s_o, 2)
-    s_c += [core_send(s_o, 2, 1), core_send(s_o, 2, 3)]
+    s_f = x_forwards(s_o, 3)
+    s_c += [core_send(s_o, 3, 1), core_send(s_o, 3, 3)]
     preact(1)
     preact(3)
+    arrived(l_z)
+    later = {"x": x_sends(l_o, 1), "c": [core_send(l_o, 1, 0)]}
     arrived(s_f)
-    s_c.append(core_send(s_o, 2, 2))
-    arrived([l_pair])
-    l_o[c, x, z] = lpad[c] + l_rx[...]
-    l_z = z_sends(l_o, 1)
-    arrived(tok_f)
-    tok_c[2] = core_send(tok_o, 0, 2)
-    arrived(s_c)
-
-    later = {}
-
-    def lost_x():
-        arrived(l_z)
-        later["x"] = x_sends(l_o, 1)
-        later["c"] = [core_send(l_o, 1, 0)]
+    s_c.append(core_send(s_o, 3, 2))
+
+    def tokens_last():
+        tok_c[2] = []
+        for h in range(2):
+            arrived(tok_f[h])
+            tok_c[2].append(core_send(tok_o.at[h], 2 * h, 2))
 
     def lost_forward():
         arrived(later["x"])
@@ -345,23 +354,29 @@
         damping = s_o[0, 2 * i : 2 * i + 2, :, :, 256:].reshape(HALF, 128).astype(F32)
         return jnp.where(eye, damping[:, 0:1] + damping[:, 1:2], 0.0)
 
+    tokens_last()
+    arrived(s_c)
     xy[HALF:, :] = s_block(0, 0).astype(F32) + diagonal(0)
-    tasks = {
-        0: [lambda: preact(2)], 1: [lost_x], 2: [lambda: gated(0)], 4: [lambda: gated(1), lambda: gated(3)],
-        5: [lost_forward], 7: [lambda: gated(2), gather_rows],
+    tasks = {1: [lambda: preact(2)], 4: [lambda: gated(0)]}
+    more_tasks = {
+        0: [lost_forward, lambda: gated(1)], 1: [lambda: gated(3)], 5: [lambda: gated(2)], 6: [lost_last],
     }
 
-    def first_tasks(step):
-        for task in tasks.get(step, []):
-            task()
-
-    newton(xy, first_tasks)
+    def between(plan):
+        def run(step):
+            for task in plan.get(step, []):
+                task()
+
+        return run
+
+    newton(xy, between(tasks))
+    gather_rows()
     inv[...] = xy[:HALF, :]
     a_inv = split(inv[...])
     b_block = s_block(0, 1)
     v = dot(s_block(1, 0), a_inv[0]) + dot(s_block(1, 0), a_inv[1])
     xy[HALF:, :] = s_block(1, 1).astype(F32) + diagonal(1) - dot2(split(v), b_block)
-    newton(xy, lambda step: lost_last() if step == 1 else None)
+    newton(xy, between(more_tasks))
     e_inv = split(xy[:HALF, :])
     arrived([slabd, later["s"]])
     rows[WIDTH:] = slabh_o[...].astype(F32)
@@ -380,28 +395,35 @@
 
     scale = FF ** (-0.5)
     order = (2, 1, 3, 0)
-    mine = pl.ds(pl.multiple_of(c * 1024, 1024), 1024)
-    theirs = pl.ds(pl.multiple_of(other * 1024, 1024), 1024)
-    pairs = {}
+    low, top = pl.ds(0, 64), pl.ds(64, 64)
+    pairs, to_right, to_left, plain, summed = {}, [], [], [], []
     for k in order:
         arrived(shares[k])
-        ptx[k] = (dot(hid[k].reshape(128, WIDTH), corr[:, theirs]) * scale).astype(BF)
-        pairs[k] = send(ptx.at[k], prx.at[k], p_s.at[k], p_r.at[k], partner)
-    for k in order:
-        own[k] = dot(hid[k].reshape(128, WIDTH), corr[:, mine]) * scale
-    arrived([pairs[2]])
-    x2[...] = (own[2] + prx[2].astype(F32)).astype(BF)
-    low, top = pl.ds(0, 64), pl.ds(64, 64)
-    to_right = send(x2.at[low], xa, a_s.at[0], a_r.at[0], right)
-    to_left = send(x2.at[top], xb, a_s.at[1], a_r.at[1], left)
-    arrived([pairs[1]])
-    own[1] = own[1] + prx[1].astype(F32)
-    xtx[0, 64:] = own[1, 64:].astype(BF)
-    plain = [send(xtx.at[0, top], xrx.at[0, top], e_s.at[0], e_r.at[0], right)]
-    arrived([pairs[3]])
-    own[3] = own[3] + prx[3].astype(F32)
-    xtx[1, :64] = own[3, :64].astype(BF)
-    plain.append(send(xtx.at[1, low], xrx.at[1, low], e_s.at[1], e_r.at[1], left))
+
+    def product(k, core, h):
+        cols = pl.ds(pl.multiple_of(core * 1024 + h * 512, 512), 512)
+        return dot(hid[k].reshape(128, WIDTH), corr[:, cols]) * scale
+
+    for h in range(2):
+        for k in order:
+            ptx[h, k] = product(k, other, h).astype(BF)
+            pairs[h, k] = send(ptx.at[h, k], prx.at[h, k], p_s.at[h, k], p_r.at[h, k], partner)
+        for k in order:
+            own[h, k] = product(k, c, h)
+        arrived([pairs[h, 2]])
+        x2[h] = (own[h, 2] + prx[h, 2].astype(F32)).astype(BF)
+        to_right.append(send(x2.at[h, low], xa.at[h], a_s.at[h, 0], a_r.at[h, 0], right))
+        to_left.append(send(x2.at[h, top], xb.at[h], a_s.at[h, 1], a_r.at[h, 1], left))
+        arrived([pairs[h, 1]])
+        own[h, 1] = own[h, 1] + prx[h, 1].astype(F32)
+        xtx[h, 0, 64:] = own[h, 1, 64:].astype(BF)
+        here, there = xtx.at[h, 0, top], xrx.at[h, 0, top]
+        plain.append([send(here, there, e_s.at[h, 0], e_r.at[h, 0], right)])
+        arrived([pairs[h, 3]])
+        own[h, 3] = own[h, 3] + prx[h, 3].astype(F32)
+        xtx[h, 1, :64] = own[h, 3, :64].astype(BF)
+        here, there = xtx.at[h, 1, low], xrx.at[h, 1, low]
+        plain[h].append(send(here, there, e_s.at[h, 1], e_r.at[h, 1], left))
 
     even = (pair * 2 + 1) * WIDTH
     even_kept = WIDTH
@@ -418,43 +440,76 @@
     row = lax.broadcasted_iota(jnp.int32, (KEPT, 16), 0)
     slab_pack = jnp.where(row == slab_goal, 1.0, 0.0).astype(BF)
 
+    stored = []
+
     def packed(half):
         cols = pl.ds(half * 1024, 1024)
-        pruned_o[:, cols] = (dot(pack, corr[:, cols]) + dot(slab_pack, slabc[:, cols])).astype(BF)
-
-    packed(0)
-    arrived([to_right])
-    xtx[0, :64] = (own[1, :64] + xa[...].astype(F32)).astype(BF)
-    summed = [send(xtx.at[0, low], xrx.at[0, low], e_s.at[2], e_r.at[2], right)]
-    arrived([to_left])
-    xtx[1, 64:] = (own[3, 64:] + xb[...].astype(F32)).astype(BF)
-    summed.append(send(xtx.at[1, top], xrx.at[1, top], e_s.at[3], e_r.at[3], left))
-    packed(1)
-    arrived([pairs[0]])
-    total = own[0] + prx[0].astype(F32)
-    arrived(plain + summed)
-    own[0] = total + xrx[0].astype(F32) + xrx[1].astype(F32)
-
-    def z_rows(k):
+        packed_v[half] = (dot(pack, corr[:, cols]) + dot(slab_pack, slabc[:, cols])).astype(BF)
+        for k in range(4):
+            there = pruned_o.at[:, pl.ds(half * 1024 + k * 256, 256)]
+            copy = pltpu.make_async_copy(packed_v.at[half, :, pl.ds(k * 256, 256)], there, out_s.at[half, k])
+            copy.start()
+            stored.append(copy)
+
+    for h in range(2):
+        arrived([to_right[h]])
+        xtx[h, 0, :64] = (own[h, 1, :64] + xa[h].astype(F32)).astype(BF)
+        here, there = xtx.at[h, 0, low], xrx.at[h, 0, low]
+        summed.append([send(here, there, e_s.at[h, 2], e_r.at[h, 2], right)])
+        arrived([to_left[h]])
+        xtx[h, 1, 64:] = (own[h, 3, 64:] + xb[h].astype(F32)).astype(BF)
+        here, there = xtx.at[h, 1, top], xrx.at[h, 1, top]
+        summed[h].append(send(here, there, e_s.at[h, 3], e_r.at[h, 3], left))
+        packed(h)
+
+    def z_rows(h, k):
         start = pl.multiple_of(((z + k) % NZ) * 8, 8)
-        return jnp.concatenate([own[0, pl.ds(start, 8)], own[0, pl.ds(64 + start, 8)]], axis=0)
-
-    zs = []
-    for k in range(1, NZ):
-        ztx[k - 1] = z_rows(k).astype(BF)
-        zs.append(send(ztx.at[k - 1], zrx.at[k - 1], w_s.at[k - 1], w_r.at[k - 1], zdev[k - 1]))
-    total = z_rows(0)
-    for k in range(NZ - 1):
-        arrived([zs[k]])
-        total = total + zrx[k].astype(F32)
-    fin[0] = total[:8]
-    fin[1] = total[8:]
+        return jnp.concatenate([own[h, 0, pl.ds(start, 8)], own[h, 0, pl.ds(64 + start, 8)]], axis=0)
+
+    zs = {}
+    for h in range(2):
+        arrived([pairs[h, 0]])
+        total = own[h, 0] + prx[h, 0].astype(F32)
+        arrived(plain[h] + summed[h])
+        own[h, 0] = total + xrx[h, 0].astype(F32) + xrx[h, 1].astype(F32)
+        for k in range(1, NZ):
+            ztx[h, k - 1] = z_rows(h, k).astype(BF)
+            here, there = ztx.at[h, k - 1], zrx.at[h, k - 1]
+            zs[h, k] = send(here, there, w_s.at[h, k - 1], w_r.at[h, k - 1], zdev[k - 1])
+    for h in range(2):
+        total = z_rows(h, 0)
+        for k in range(1, NZ):
+            arrived([zs[h, k]])
+            total = total + zrx[h, k - 1].astype(F32)
+        fin[0, :, h * 512 : h * 512 + 512] = total[:8]
+        fin[1, :, h * 512 : h * 512 + 512] = total[8:]
     last = send(fin.at[other], frx, f_s.at[0], f_r.at[0], partner)
+    mine = pl.ds(pl.multiple_of(c * 1024, 1024), 1024)
+    theirs = pl.ds(pl.multiple_of(other * 1024, 1024), 1024)
     mixed_o[:, mine] = fin[c].astype(BF)
     arrived([last])
     mixed_o[:, theirs] = frx[...].astype(BF)
+    for copy in stored:
+        copy.wait()
     for copy in pending:
         copy.wait_send()
+
+
+def hand_over_kernel(pruned, mixed, pruned_o, mixed_o, pruned_v, mixed_v, in_s, out_s):
+    parts = []
+    for k in range(PIECES):
+        cols = pl.ds(k * (2048 // PIECES), 2048 // PIECES)
+        parts.append((pruned.at[:, cols], pruned_v.at[k], pruned_o.at[:, cols]))
+    parts.append((mixed, mixed_v, mixed_o))
+    arriving = [pltpu.make_async_copy(src, mid, in_s.at[k]) for k, (src, mid, _) in enumerate(parts)]
+    leaving = [pltpu.make_async_copy(mid, dst, out_s.at[k]) for k, (_, mid, dst) in enumerate(parts)]
+    for copy in arriving:
+        copy.start()
+    for into, copy in zip(arriving, leaving):
+        into.wait()
+        copy.start()
+    for copy in leaving:
+        copy.wait()
 
 
 def dma(*shape):
@@ -480,26 +535,27 @@
     def f32(*shape):
         return pltpu.VMEM(shape, F32)
 
-    return pl.pallas_call(
+    pruned, mixed = pl.pallas_call(
         prune_kernel,
         out_shape=(out(KEPT, 2048), out(8, 2048)),
         in_specs=[pl.BlockSpec(memory_space=pltpu.SMEM)] + [hbm()] * 7,
-        out_specs=(vmem(), vmem()),
+        out_specs=(hbm(), vmem()),
         scratch_shapes=[
             bf(8, 2048), bf(WIDTH, 2048), f32(FF // 128, 128), pltpu.VMEM((4, 128), jnp.int32),
             bf(4, BLOCK, FF // 4), bf(2 * WIDTH, 2048),
-            bf(2, NX, NZ, 16, 1024), bf(2, NX, NZ, 16, 1024), bf(2, NX, NZ, 16, 384),
+            bf(2, 2, NX, NZ, 16, 512), bf(2, NX, NZ, 16, 1024), bf(2, NX, NZ, 16, 384),
             bf(NY, BLOCK, REM), bf(16, 2048), bf(16, REM),
             bf(2, 16, 1024), bf(2, 16, 384), bf(16, 1024), bf(7, 16, 384), bf(16, 2048), bf(16, REM),
             bf(2, 128, 1024), f32(128, 2 * WIDTH), bf(4, 3, 32, 2 * WIDTH), bf(4, 3, 32, 2 * WIDTH),
             f32(4, 32, 2 * WIDTH), bf(4, NY, 32, WIDTH),
             f32(2 * HALF, HALF), f32(HALF, HALF), f32(WIDTH + 16, REM), bf(WIDTH, 2048), bf(16, 2048),
-            bf(4, 128, 1024), bf(4, 128, 1024), f32(4, 128, 1024), bf(128, 1024), bf(64, 1024), bf(64, 1024),
-            bf(2, 128, 1024), bf(2, 128, 1024), bf(7, 16, 1024), bf(7, 16, 1024), f32(2, 8, 1024), f32(8, 1024),
-            dma(6), dma(4), dma(1), dma(1), dma(7), dma(7), dma(3), dma(3), dma(3, 7), dma(3, 7),
-            dma(3, 4), dma(3, 4), dma(3, 4), dma(3, 4), dma(2), dma(2),
+            bf(2, 4, 128, 512), bf(2, 4, 128, 512), f32(2, 4, 128, 512), bf(2, 128, 512), bf(2, 64, 512), bf(2, 64, 512),
+            bf(2, 2, 128, 512), bf(2, 2, 128, 512), bf(2, 7, 16, 512), bf(2, 7, 16, 512), f32(2, 8, 1024), f32(8, 1024),
+            dma(6), dma(4), dma(1), dma(1), dma(7), dma(7), dma(3), dma(3), dma(4, 7), dma(4, 7),
+            dma(4, 4), dma(4, 4), dma(4, 4), dma(4, 4), dma(2), dma(2),
             dma(4, 3), dma(4, 3), dma(4, 3), dma(4, 3),
-            dma(4), dma(4), dma(2), dma(2), dma(4), dma(4), dma(7), dma(7), dma(1), dma(1),
+            dma(2, 4), dma(2, 4), dma(2, 2), dma(2, 2), dma(2, 4), dma(2, 4), dma(2, 7), dma(2, 7), dma(1), dma(1),
+            bf(2, KEPT, 1024), dma(2, 4),
         ],
         compiler_params=pltpu.CompilerParams(
             collective_id=1, has_side_effects=True, vmem_limit_bytes=VMEM_LIMIT
@@ -509,6 +565,17 @@
         removed, tokens, gate_weight.T, up_weight.T, down_weight, inverse_hessian,
         damping.reshape(FF // 128, 128), removed.reshape(4, 128),
     )
+    return pl.pallas_call(
+        hand_over_kernel,
+        out_shape=(out(KEPT, 2048), out(8, 2048)),
+        in_specs=[hbm(), hbm()],
+        out_specs=(hbm(), hbm()),
+        scratch_shapes=[
+            bf(PIECES, KEPT, 2048 // PIECES), bf(8, 2048), dma(PIECES + 1), dma(PIECES + 1),
+        ],
+        compiler_params=pltpu.CompilerParams(vmem_limit_bytes=VMEM_LIMIT),
+        name="hand_over",
+    )(pruned, mixed)
 
 
 def solution(mesh):

time: 90.9 us -> 76.5 us (0.84)
  Pallas kernels: 85.8 us -> 75.5 us
  local copies, waits for them, and re-layouts: 3.44 us -> 0 us
    pallas_call x1, Pallas kernels: 85.8 us -> 73.1 us  [shards(): pl.pallas_call(prune_kernel, out_shape=(out(KEPT, 2048), out(8, 2048)), i...]
    unnamed x4 -> x0, local copies, waits for them, and re-layouts: 3.44 us -> none
    pallas_call x0 -> x1, Pallas kernels: none -> 2.37 us  [shards(): pl.pallas_call(hand_over_kernel, out_shape=(out(KEPT, 2048), out(8, 2048)...]
where the time goes in v3:
time: 76.5 us; the launch traced here: 76.3 us
  Pallas kernels  75.5 us (99%)
  between operations  0.8 us (1%)
    pallas_call x1, Pallas kernels, shards(): pl.pallas_call(prune_kernel, out_shape=(out(KEPT, 2048), out(8, 2048)), i...  73.1 us
    pallas_call x1, Pallas kernels, shards(): pl.pallas_call(hand_over_kernel, out_shape=(out(KEPT, 2048), out(8, 2048)...  2.37 us

profile of v3, /device:TPU:1, one launch (start us, length us, event | category | flops | bytes accessed | tf_op | source)
XLA Modules:
  0.0 76.3 jit_solution(9374106356998161519)
XLA Ops:
  0.6 73.1 %prune.1 = (bf16[408,2048]{1,0:T(8,128)(2,1)}, bf16[8,2048]{1,0:T(8,128)(2,1)}) custom-call(s32[512]{0:T(512)} %removed_s.1, bf16[8,2048]{1,0:T(8,128)(2,1)} %tok_h.1, bf16[416,2048]{1,0:T(8,128)(2,1)} %bitcast.4, bf16[416,2048]{1,0:T(8,128)(2,1)} %bitcast.5, bf16[416,2048]{1,0:T(8,128)(2,1)} %down_h.1, bf16[104,26624]{1,0:T(8,128)(2,1)} %hess_h.1, ...), custom_call_target="tpu_custom_call" | custom-call | tf_op jit(solution)/shard_map/prune/pallas_call | solution.py:538
  73.8 2.4 %hand_over.1 = (bf16[408,2048]{1,0:T(8,128)(2,1)}, bf16[8,2048]{1,0:T(8,128)(2,1)}) custom-call(bf16[408,2048]{1,0:T(8,128)(2,1)} %get-tuple-element.4.pruned, bf16[8,2048]{1,0:T(8,128)(2,1)} %get-tuple-element.5.mixed), custom_call_target="tpu_custom_call" | custom-call | tf_op jit(solution)/shard_map/hand_over/pallas_call | solution.py:568

commit v4 on v3

--- a/solution.py
+++ b/solution.py
@@ -14,9 +14,10 @@
 KEPT = 408
 FF = 26624
 REM = 512
-STEPS = 8
+STEPS = 7
 HALF = REM // 2
 PIECES = 8
+SPLIT = 4
 VMEM_LIMIT = 56 * 1024 * 1024
 
 
@@ -57,10 +58,6 @@
     for j, r in enumerate(indices):
         out = jnp.where(row == j, r, out)
     return out
-
-
-def dot_nt(a, b):
-    return lax.dot_general(a, b, (((1,), (1,)), ((), ())), preferred_element_type=F32)
 
 
 def ranks(indices, first, offset, lanes, rows=16):
@@ -93,7 +90,7 @@
     square = xy[n:, :]
     bound = jnp.max(jnp.sum(jnp.abs(square), axis=0, keepdims=True), axis=1, keepdims=True)
     inverse_bound = 1.0 / bound
-    low = 0.5 * inverse_bound
+    low = 0.9 * inverse_bound
     xy[n:, :] = square * inverse_bound
     for step in range(STEPS):
         middle = 0.5 * (1.0 + low)
@@ -116,14 +113,14 @@
     removed_s, tok_h, gate_h, up_h, down_h, hess_h, damp_h, removed_h,
     pruned_o, mixed_o,
     tok_in, down, damp, removed_v, hbuf, weight,
-    tok_o, l_o, s_o, hkr_o, slabd_o, slabh_o,
+    tok_o, l_a, l_b, s_o, hkr_o, slabd_o, slabh_o,
     lpad, spad, l_rx, s_rx, slabd_tx, slabh_tx,
     lhs, pre, pre_tx, pre_rx, pre_own, hid,
     xy, inv, rows, corr, slabc,
-    ptx, prx, own, x2, xa, xb, xtx, xrx, ztx, zrx, fin, frx,
+    ptx, prx, own, x2, xa, xb, xtx, xrx, ztx, zrx,
     load_s, hess_s, pair_s, pair_r, sc_s, sc_r, y_s, y_r, z_s, z_r, x_s, x_r, c_s, c_r, sl_s, sl_r,
     ps_s, ps_r, h_s, h_r,
-    p_s, p_r, a_s, a_r, e_s, e_r, w_s, w_r, f_s, f_r, packed_v, out_s,
+    p_s, p_r, a_s, a_r, e_s, e_r, w_s, w_r, packed_v, out_s, turned, lx_s, lx_r,
 ):
     x, z, c, d = place()
     other = 1 - c
@@ -148,8 +145,9 @@
     right, left = at((x + 1) % NX, z, c, d), at((x + 3) % NX, z, c, d)
     ydev = [at(x, z, c, (d + k) % NY) for k in range(1, NY)]
     ycross = [at(x, z, other, (d + k) % NY) for k in range(1, NY)]
+    across = at((x + 2) % NX, z, c, d)
     zdev = [at(x, (z + k) % NZ, c, d) for k in range(1, NZ)]
-    greet([partner, right, left] + ydev + ycross + zdev)
+    greet([partner, right, left, across] + ydev + ycross + zdev)
     pending = []
 
     def send(src, dst, s, r, device):
@@ -246,6 +244,10 @@
     slabd_tx[...] = dot(slab_pick.astype(BF), down[...]).astype(BF)
     slabd = send(slabd_tx, slabd_o, sl_s.at[0], sl_r.at[0], partner)
 
+    gate_load.wait()
+    up_load.wait()
+    for i in range(4):
+        turned[512 * i : 512 * i + 512] = weight[:, 512 * i : 512 * i + 512].T
     arrived(s_sends)
     total = spad[c].astype(F32)
     for k in range(7):
@@ -253,13 +255,20 @@
     s_o[c, x, z] = total.astype(BF)
     s_z = z_sends(s_o, 3)
     arrived([l_pair])
-    l_o[c, x, z] = lpad[c] + l_rx[...]
+    value = lpad[c] + l_rx[...]
+    l_a[c, x, z] = value[:, :512]
+    l_b[c, z, x] = value[:, 512:]
+    here = l_b.at[c, z, x]
+    lb_x = [send(here, here, lx_s.at[k], lx_r.at[k], (right, across, left)[k]) for k in range(3)]
     tok_x = []
     for h in range(2):
         arrived(tok_z[h])
         tok_x.append(x_sends(tok_o.at[h], 2 * h))
     tok_c = {0: [core_send(tok_o.at[h], 2 * h, 0) for h in range(2)]}
-    l_z = z_sends(l_o, 1)
+    l_z = z_sends(l_a, 1)
+    arrived(lb_x)
+    here = l_b.at[c, z]
+    lb_z = [send(here, here, z_s.at[4, k], z_r.at[4, k], zdev[k]) for k in range(NZ - 1)]
     arrived(s_z)
     s_x = x_sends(s_o, 3)
     s_c = [core_send(s_o, 3, 0)]
@@ -275,7 +284,7 @@
                 cols = slice(h * 512, h * 512 + 512)
                 lhs[0, core * 64 : core * 64 + 64, cols] = value[:, :8].reshape(64, 512).astype(BF)
                 lhs[1, core * 64 : core * 64 + 64, cols] = value[:, 8:].reshape(64, 512).astype(BF)
-        pre[...] = dot_nt(lhs[0], weight[:, :1024]) + dot_nt(lhs[1], weight[:, 1024:])
+        pre[...] = dot(lhs[0], turned[:1024]) + dot(lhs[1], turned[1024:])
         sends = []
         for m in range(NY - 1):
             part = pl.ds(pl.multiple_of(((d + 1 + m) % NY) * 32, 32), 32)
@@ -296,12 +305,10 @@
         hidden = gate / (1.0 + jnp.exp(-gate)) * up
         for r in indices:
             hidden = jnp.where(lane == r, 0.0, hidden)
-        hid[k, d] = hidden.astype(BF)
-        here = hid.at[k, d]
+        hid[d // 2, k, d % 2] = hidden.astype(BF)
+        here = hid.at[d // 2, k, d % 2]
         shares[k] = [send(here, here, h_s.at[k, m], h_r.at[k, m], ydev[m]) for m in range(NY - 1)]
 
-    gate_load.wait()
-    up_load.wait()
     preact(0)
     tok_f = []
     tok_c[1], tok_c[3] = [], []
@@ -314,11 +321,11 @@
     s_f = x_forwards(s_o, 3)
     s_c += [core_send(s_o, 3, 1), core_send(s_o, 3, 3)]
     preact(1)
+    arrived(s_f)
+    s_c.append(core_send(s_o, 3, 2))
     preact(3)
     arrived(l_z)
-    later = {"x": x_sends(l_o, 1), "c": [core_send(l_o, 1, 0)]}
-    arrived(s_f)
-    s_c.append(core_send(s_o, 3, 2))
+    later = {"x": x_sends(l_a, 1), "c": [core_send(l_a, 1, 0)]}
 
     def tokens_last():
         tok_c[2] = []
@@ -328,12 +335,16 @@
 
     def lost_forward():
         arrived(later["x"])
-        later["f"] = x_forwards(l_o, 1)
-        later["c"] += [core_send(l_o, 1, 1), core_send(l_o, 1, 3)]
+        later["f"] = x_forwards(l_a, 1)
+        later["c"] += [core_send(l_a, 1, 1), core_send(l_a, 1, 3)]
+
+    def lost_other():
+        arrived(lb_z)
+        later["c"].append(send(l_b.at[c], l_b.at[c], c_s.at[4, 0], c_r.at[4, 0], partner))
 
     def lost_last():
         arrived(later["f"])
-        later["c"].append(core_send(l_o, 1, 2))
+        later["c"].append(core_send(l_a, 1, 2))
 
     def gather_rows():
         arrived(h_sends)
@@ -357,9 +368,9 @@
     tokens_last()
     arrived(s_c)
     xy[HALF:, :] = s_block(0, 0).astype(F32) + diagonal(0)
-    tasks = {1: [lambda: preact(2)], 4: [lambda: gated(0)]}
+    tasks = {1: [lambda: preact(2)], 4: [lambda: gated(0)], 6: [lost_forward, lambda: gated(1)]}
     more_tasks = {
-        0: [lost_forward, lambda: gated(1)], 1: [lambda: gated(3)], 5: [lambda: gated(2)], 6: [lost_last],
+        0: [lambda: gated(3)], 2: [lost_other], 3: [lambda: gated(2)], 5: [lost_last],
     }
 
     def between(plan):
@@ -383,45 +394,46 @@
     q = dot(rows[:, :HALF].astype(BF), a_inv[0]) + dot(rows[:, :HALF].astype(BF), a_inv[1])
     u = rows[:, HALF:] - dot2(split(q), b_block)
     second = dot3(split(u), e_inv)
-    pair_first = split(q - dot3(split(second), split(v)))
-    pair_second = split(second)
+    coef = [(q - dot3(split(second), split(v))).astype(BF), second.astype(BF)]
     arrived(later["c"])
-    lost_all = [l_o[h].reshape(REM, 1024) for h in range(2)]
     for half in range(2):
-        cols = pl.ds(half * 1024, 1024)
-        change = dot2(pair_first, lost_all[half][:HALF]) + dot2(pair_second, lost_all[half][HALF:])
-        corr[:, cols] = (down[:, cols].astype(F32) - change[:WIDTH]).astype(BF)
-        slabc[:, cols] = (slabd_o[:, cols].astype(F32) - change[WIDTH:]).astype(BF)
-
+        first_rows = l_a[half].reshape(REM, 512)
+        other_rows = jnp.concatenate([l_b[half, :, k].reshape(128, 512) for k in range(NX)], axis=0)
+        for piece, lost_rows in enumerate((first_rows, other_rows)):
+            cols = pl.ds(half * 1024 + piece * 512, 512)
+            change = dot(coef[0], lost_rows[:HALF]) + dot(coef[1], lost_rows[HALF:])
+            corr[:, cols] = (down[:, cols].astype(F32) - change[:WIDTH]).astype(BF)
+            slabc[:, cols] = (slabd_o[:, cols].astype(F32) - change[WIDTH:]).astype(BF)
+
+    wide = 2048 // SPLIT
     scale = FF ** (-0.5)
     order = (2, 1, 3, 0)
-    low, top = pl.ds(0, 64), pl.ds(64, 64)
+    low, top = pl.ds(0, 32), pl.ds(32, 32)
     pairs, to_right, to_left, plain, summed = {}, [], [], [], []
     for k in order:
         arrived(shares[k])
 
-    def product(k, core, h):
-        cols = pl.ds(pl.multiple_of(core * 1024 + h * 512, 512), 512)
-        return dot(hid[k].reshape(128, WIDTH), corr[:, cols]) * scale
-
-    for h in range(2):
+    def product(core, h):
+        cols = pl.ds(h * wide, wide)
+        return dot(hid[core].reshape(256, WIDTH), corr[:, cols]) * scale
+
+    for h in range(SPLIT):
+        ptx[h] = product(other, h).reshape(4, 64, wide).astype(BF)
         for k in order:
-            ptx[h, k] = product(k, other, h).astype(BF)
             pairs[h, k] = send(ptx.at[h, k], prx.at[h, k], p_s.at[h, k], p_r.at[h, k], partner)
-        for k in order:
-            own[h, k] = product(k, c, h)
+        own[h] = product(c, h).reshape(4, 64, wide)
         arrived([pairs[h, 2]])
         x2[h] = (own[h, 2] + prx[h, 2].astype(F32)).astype(BF)
         to_right.append(send(x2.at[h, low], xa.at[h], a_s.at[h, 0], a_r.at[h, 0], right))
         to_left.append(send(x2.at[h, top], xb.at[h], a_s.at[h, 1], a_r.at[h, 1], left))
         arrived([pairs[h, 1]])
         own[h, 1] = own[h, 1] + prx[h, 1].astype(F32)
-        xtx[h, 0, 64:] = own[h, 1, 64:].astype(BF)
+        xtx[h, 0, 32:] = own[h, 1, 32:].astype(BF)
         here, there = xtx.at[h, 0, top], xrx.at[h, 0, top]
         plain.append([send(here, there, e_s.at[h, 0], e_r.at[h, 0], right)])
         arrived([pairs[h, 3]])
         own[h, 3] = own[h, 3] + prx[h, 3].astype(F32)
-        xtx[h, 1, :64] = own[h, 3, :64].astype(BF)
+        xtx[h, 1, :32] = own[h, 3, :32].astype(BF)
         here, there = xtx.at[h, 1, low], xrx.at[h, 1, low]
         plain[h].append(send(here, there, e_s.at[h, 1], e_r.at[h, 1], left))
 
@@ -451,23 +463,24 @@
             copy.start()
             stored.append(copy)
 
-    for h in range(2):
+    for h in range(SPLIT):
         arrived([to_right[h]])
-        xtx[h, 0, :64] = (own[h, 1, :64] + xa[h].astype(F32)).astype(BF)
+        xtx[h, 0, :32] = (own[h, 1, :32] + xa[h].astype(F32)).astype(BF)
         here, there = xtx.at[h, 0, low], xrx.at[h, 0, low]
         summed.append([send(here, there, e_s.at[h, 2], e_r.at[h, 2], right)])
         arrived([to_left[h]])
-        xtx[h, 1, 64:] = (own[h, 3, 64:] + xb[h].astype(F32)).astype(BF)
+        xtx[h, 1, 32:] = (own[h, 3, 32:] + xb[h].astype(F32)).astype(BF)
         here, there = xtx.at[h, 1, top], xrx.at[h, 1, top]
         summed[h].append(send(here, there, e_s.at[h, 3], e_r.at[h, 3], left))
-        packed(h)
+        if h % (SPLIT // 2) == 0:
+            packed(h // (SPLIT // 2))
 
     def z_rows(h, k):
-        start = pl.multiple_of(((z + k) % NZ) * 8, 8)
-        return jnp.concatenate([own[h, 0, pl.ds(start, 8)], own[h, 0, pl.ds(64 + start, 8)]], axis=0)
+        value = own[h, 0, pl.ds(pl.multiple_of(((z + k) % NZ) * 8, 8), 8)]
+        return jnp.concatenate([value[:, : wide // 2], value[:, wide // 2 :]], axis=0)
 
     zs = {}
-    for h in range(2):
+    for h in range(SPLIT):
         arrived([pairs[h, 0]])
         total = own[h, 0] + prx[h, 0].astype(F32)
         arrived(plain[h] + summed[h])
@@ -476,19 +489,13 @@
             ztx[h, k - 1] = z_rows(h, k).astype(BF)
             here, there = ztx.at[h, k - 1], zrx.at[h, k - 1]
             zs[h, k] = send(here, there, w_s.at[h, k - 1], w_r.at[h, k - 1], zdev[k - 1])
-    for h in range(2):
+    for h in range(SPLIT):
         total = z_rows(h, 0)
         for k in range(1, NZ):
             arrived([zs[h, k]])
             total = total + zrx[h, k - 1].astype(F32)
-        fin[0, :, h * 512 : h * 512 + 512] = total[:8]
-        fin[1, :, h * 512 : h * 512 + 512] = total[8:]
-    last = send(fin.at[other], frx, f_s.at[0], f_r.at[0], partner)
-    mine = pl.ds(pl.multiple_of(c * 1024, 1024), 1024)
-    theirs = pl.ds(pl.multiple_of(other * 1024, 1024), 1024)
-    mixed_o[:, mine] = fin[c].astype(BF)
-    arrived([last])
-    mixed_o[:, theirs] = frx[...].astype(BF)
+        mixed_o[:, h * wide : h * wide + wide // 2] = total[:8].astype(BF)
+        mixed_o[:, h * wide + wide // 2 : (h + 1) * wide] = total[8:].astype(BF)
     for copy in stored:
         copy.wait()
     for copy in pending:
@@ -529,6 +536,8 @@
 
 
 def shards(tokens, gate_weight, up_weight, down_weight, inverse_hessian, damping, removed):
+    wide = 2048 // SPLIT
+
     def bf(*shape):
         return pltpu.VMEM(shape, BF)
 
@@ -543,19 +552,22 @@
         scratch_shapes=[
             bf(8, 2048), bf(WIDTH, 2048), f32(FF // 128, 128), pltpu.VMEM((4, 128), jnp.int32),
             bf(4, BLOCK, FF // 4), bf(2 * WIDTH, 2048),
-            bf(2, 2, NX, NZ, 16, 512), bf(2, NX, NZ, 16, 1024), bf(2, NX, NZ, 16, 384),
+            bf(2, 2, NX, NZ, 16, 512), bf(2, NX, NZ, 16, 512), bf(2, NZ, NX, 16, 512), bf(2, NX, NZ, 16, 384),
             bf(NY, BLOCK, REM), bf(16, 2048), bf(16, REM),
             bf(2, 16, 1024), bf(2, 16, 384), bf(16, 1024), bf(7, 16, 384), bf(16, 2048), bf(16, REM),
             bf(2, 128, 1024), f32(128, 2 * WIDTH), bf(4, 3, 32, 2 * WIDTH), bf(4, 3, 32, 2 * WIDTH),
-            f32(4, 32, 2 * WIDTH), bf(4, NY, 32, WIDTH),
+            f32(4, 32, 2 * WIDTH), bf(2, 4, 2, 32, WIDTH),
             f32(2 * HALF, HALF), f32(HALF, HALF), f32(WIDTH + 16, REM), bf(WIDTH, 2048), bf(16, 2048),
-            bf(2, 4, 128, 512), bf(2, 4, 128, 512), f32(2, 4, 128, 512), bf(2, 128, 512), bf(2, 64, 512), bf(2, 64, 512),
-            bf(2, 2, 128, 512), bf(2, 2, 128, 512), bf(2, 7, 16, 512), bf(2, 7, 16, 512), f32(2, 8, 1024), f32(8, 1024),
-            dma(6), dma(4), dma(1), dma(1), dma(7), dma(7), dma(3), dma(3), dma(4, 7), dma(4, 7),
-            dma(4, 4), dma(4, 4), dma(4, 4), dma(4, 4), dma(2), dma(2),
+            bf(SPLIT, 4, 64, wide), bf(SPLIT, 4, 64, wide), f32(SPLIT, 4, 64, wide),
+            bf(SPLIT, 64, wide), bf(SPLIT, 32, wide), bf(SPLIT, 32, wide),
+            bf(SPLIT, 2, 64, wide), bf(SPLIT, 2, 64, wide),
+            bf(SPLIT, 7, 16, wide // 2), bf(SPLIT, 7, 16, wide // 2),
+            dma(6), dma(4), dma(1), dma(1), dma(7), dma(7), dma(3), dma(3), dma(5, 7), dma(5, 7),
+            dma(4, 4), dma(4, 4), dma(5, 4), dma(5, 4), dma(2), dma(2),
             dma(4, 3), dma(4, 3), dma(4, 3), dma(4, 3),
-            dma(2, 4), dma(2, 4), dma(2, 2), dma(2, 2), dma(2, 4), dma(2, 4), dma(2, 7), dma(2, 7), dma(1), dma(1),
-            bf(2, KEPT, 1024), dma(2, 4),
+            dma(SPLIT, 4), dma(SPLIT, 4), dma(SPLIT, 2), dma(SPLIT, 2), dma(SPLIT, 4), dma(SPLIT, 4),
+            dma(SPLIT, 7), dma(SPLIT, 7),
+            bf(2, KEPT, 1024), dma(2, 4), bf(2048, 2 * WIDTH), dma(3), dma(3),
         ],
         compiler_params=pltpu.CompilerParams(
             collective_id=1, has_side_effects=True, vmem_limit_bytes=VMEM_LIMIT

time: 76.5 us -> 74.2 us (0.970); the launches traced: 76.3 us -> 72.9 us
  Pallas kernels: 75.5 us -> 72.1 us
    pallas_call x1, Pallas kernels: 73.1 us -> 69.7 us  [shards(): pl.pallas_call(prune_kernel, out_shape=(out(KEPT, 2048), out(8, 2048)), i...]
where the time goes in v4:
time: 74.2 us; the launch traced here: 72.9 us
  Pallas kernels  72.1 us (97%)
  between operations  0.8 us (1%)
    pallas_call x1, Pallas kernels, shards(): pl.pallas_call(prune_kernel, out_shape=(out(KEPT, 2048), out(8, 2048)), i...  69.7 us
    pallas_call x1, Pallas kernels, shards(): pl.pallas_call(hand_over_kernel, out_shape=(out(KEPT, 2048), out(8, 2048)...  2.37 us

profile of v4, /device:TPU:1, one launch (start us, length us, event | category | flops | bytes accessed | tf_op | source)
XLA Modules:
  0.0 72.9 jit_solution(10948306884180150708)
XLA Ops:
  0.6 69.7 %prune.1 = (bf16[408,2048]{1,0:T(8,128)(2,1)}, bf16[8,2048]{1,0:T(8,128)(2,1)}) custom-call(s32[512]{0:T(512)} %removed_s.1, bf16[8,2048]{1,0:T(8,128)(2,1)} %tok_h.1, bf16[416,2048]{1,0:T(8,128)(2,1)} %bitcast.4, bf16[416,2048]{1,0:T(8,128)(2,1)} %bitcast.5, bf16[416,2048]{1,0:T(8,128)(2,1)} %down_h.1, bf16[104,26624]{1,0:T(8,128)(2,1)} %hess_h.1, ...), custom_call_target="tpu_custom_call" | custom-call | tf_op jit(solution)/shard_map/prune/pallas_call | solution.py:547
  70.3 2.4 %hand_over.1 = (bf16[408,2048]{1,0:T(8,128)(2,1)}, bf16[8,2048]{1,0:T(8,128)(2,1)}) custom-call(bf16[408,2048]{1,0:T(8,128)(2,1)} %get-tuple-element.4.pruned, bf16[8,2048]{1,0:T(8,128)(2,1)} %get-tuple-element.5.mixed), custom_call_target="tpu_custom_call" | custom-call | tf_op jit(solution)/shard_map/hand_over/pallas_call | solution.py:580

commit v5 on v4

--- a/solution.py
+++ b/solution.py
@@ -421,6 +421,7 @@
         ptx[h] = product(other, h).reshape(4, 64, wide).astype(BF)
         for k in order:
             pairs[h, k] = send(ptx.at[h, k], prx.at[h, k], p_s.at[h, k], p_r.at[h, k], partner)
+    for h in range(SPLIT):
         own[h] = product(c, h).reshape(4, 64, wide)
         arrived([pairs[h, 2]])
         x2[h] = (own[h, 2] + prx[h, 2].astype(F32)).astype(BF)

time: 74.2 us -> 74.1 us (level); the launches traced: 72.9 us -> 73.9 us
  Pallas kernels: 72.1 us -> 73.1 us
    pallas_call x1, Pallas kernels: 69.7 us -> 70.8 us  [shards(): pl.pallas_call(prune_kernel, out_shape=(out(KEPT, 2048), out(8, 2048)), i...]
where the time goes in v5:
time: 74.1 us; the launch traced here: 73.9 us
  Pallas kernels  73.1 us (99%)
  between operations  0.8 us (1%)
    pallas_call x1, Pallas kernels, shards(): pl.pallas_call(prune_kernel, out_shape=(out(KEPT, 2048), out(8, 2048)), i...  70.8 us
    pallas_call x1, Pallas kernels, shards(): pl.pallas_call(hand_over_kernel, out_shape=(out(KEPT, 2048), out(8, 2048)...  2.37 us

profile of v5, /device:TPU:1, one launch (start us, length us, event | category | flops | bytes accessed | tf_op | source)
XLA Modules:
  0.0 73.9 jit_solution(2837568993262261862)
XLA Ops:
  0.6 70.8 %prune.1 = (bf16[408,2048]{1,0:T(8,128)(2,1)}, bf16[8,2048]{1,0:T(8,128)(2,1)}) custom-call(s32[512]{0:T(512)} %removed_s.1, bf16[8,2048]{1,0:T(8,128)(2,1)} %tok_h.1, bf16[416,2048]{1,0:T(8,128)(2,1)} %bitcast.4, bf16[416,2048]{1,0:T(8,128)(2,1)} %bitcast.5, bf16[416,2048]{1,0:T(8,128)(2,1)} %down_h.1, bf16[104,26624]{1,0:T(8,128)(2,1)} %hess_h.1, ...), custom_call_target="tpu_custom_call" | custom-call | tf_op jit(solution)/shard_map/prune/pallas_call | solution.py:548
  71.4 2.4 %hand_over.1 = (bf16[408,2048]{1,0:T(8,128)(2,1)}, bf16[8,2048]{1,0:T(8,128)(2,1)}) custom-call(bf16[408,2048]{1,0:T(8,128)(2,1)} %get-tuple-element.4.pruned, bf16[8,2048]{1,0:T(8,128)(2,1)} %get-tuple-element.5.mixed), custom_call_target="tpu_custom_call" | custom-call | tf_op jit(solution)/shard_map/hand_over/pallas_call | solution.py:581

commit v6 on v4

--- a/solution.py
+++ b/solution.py
@@ -472,8 +472,6 @@
         xtx[h, 1, 32:] = (own[h, 3, 32:] + xb[h].astype(F32)).astype(BF)
         here, there = xtx.at[h, 1, top], xrx.at[h, 1, top]
         summed[h].append(send(here, there, e_s.at[h, 3], e_r.at[h, 3], left))
-        if h % (SPLIT // 2) == 0:
-            packed(h // (SPLIT // 2))
 
     def z_rows(h, k):
         value = own[h, 0, pl.ds(pl.multiple_of(((z + k) % NZ) * 8, 8), 8)]
@@ -489,6 +487,8 @@
             ztx[h, k - 1] = z_rows(h, k).astype(BF)
             here, there = ztx.at[h, k - 1], zrx.at[h, k - 1]
             zs[h, k] = send(here, there, w_s.at[h, k - 1], w_r.at[h, k - 1], zdev[k - 1])
+    packed(0)
+    packed(1)
     for h in range(SPLIT):
         total = z_rows(h, 0)
         for k in range(1, NZ):

time: 74.2 us -> 74.2 us (level); the launches traced: 72.9 us -> 73.6 us
    pallas_call x1, Pallas kernels: 69.7 us -> 70.4 us  [shards(): pl.pallas_call(prune_kernel, out_shape=(out(KEPT, 2048), out(8, 2048)), i...]
where the time goes in v6:
time: 74.2 us; the launch traced here: 73.6 us
  Pallas kernels  72.8 us (98%)
  between operations  0.8 us (1%)
    pallas_call x1, Pallas kernels, shards(): pl.pallas_call(prune_kernel, out_shape=(out(KEPT, 2048), out(8, 2048)), i...  70.4 us
    pallas_call x1, Pallas kernels, shards(): pl.pallas_call(hand_over_kernel, out_shape=(out(KEPT, 2048), out(8, 2048)...  2.37 us

profile of v6, /device:TPU:1, one launch (start us, length us, event | category | flops | bytes accessed | tf_op | source)
XLA Modules:
  0.0 73.6 jit_solution(7262362076927823903)
XLA Ops:
  0.6 70.4 %prune.1 = (bf16[408,2048]{1,0:T(8,128)(2,1)}, bf16[8,2048]{1,0:T(8,128)(2,1)}) custom-call(s32[512]{0:T(512)} %removed_s.1, bf16[8,2048]{1,0:T(8,128)(2,1)} %tok_h.1, bf16[416,2048]{1,0:T(8,128)(2,1)} %bitcast.4, bf16[416,2048]{1,0:T(8,128)(2,1)} %bitcast.5, bf16[416,2048]{1,0:T(8,128)(2,1)} %down_h.1, bf16[104,26624]{1,0:T(8,128)(2,1)} %hess_h.1, ...), custom_call_target="tpu_custom_call" | custom-call | tf_op jit(solution)/shard_map/prune/pallas_call | solution.py:547
  71.1 2.4 %hand_over.1 = (bf16[408,2048]{1,0:T(8,128)(2,1)}, bf16[8,2048]{1,0:T(8,128)(2,1)}) custom-call(bf16[408,2048]{1,0:T(8,128)(2,1)} %get-tuple-element.4.pruned, bf16[8,2048]{1,0:T(8,128)(2,1)} %get-tuple-element.5.mixed), custom_call_target="tpu_custom_call" | custom-call | tf_op jit(solution)/shard_map/hand_over/pallas_call | solution.py:580
